TPU v7x, 512 devices: a whole 4x8x8 slice. The times are simulated.
512 devices in a mesh: tm: 32 (over z, y_lo), base: 16 (over x, y_hi, core).
Axes of the slice: x: 4, y: 8 (y_hi: 2, y_lo: 4; y = y_hi * 4 + y_lo), z: 8, core: 2. Of those that a mesh axis runs over, the one named last changes fastest.
Arguments:
- visibilities: bfloat16 [4096, 1024, 128], P('tm', 'base'), may hold values from -6 to 6
- pseudo_inverse: bfloat16 [512, 1024, 1024], P('tm', 'base'), may hold values from -0.25 to 0.25
- baseline_group: int32 [1024], P('base'), may hold values from 0 to 7
- group_count: int32 [512], P('tm'), may hold values from 4 to 8
Outputs:
- sky: bfloat16 [512, 512, 128], P('tm', 'base')
All inputs are finite; a program needn't handle non-finite values.
Results may differ from a plain program's by a relative error of at most 0.0055.
Values may be sent and summed in bfloat16 or wider, within the bound.
No kernel may reach another device: no remote copies, remote signals or barrier semaphores. Data moves between devices by JAX's collectives and lax.ppermute only.
A program may use at most 64 MiB of HBM per device.

v0:
```python
import math

import jax
import jax.numpy as jnp
from jax import lax
from jax.sharding import PartitionSpec as P


def twiddles(start_position, row_entries, harmonic_orders_full, sidereal_epoch_count):
    index = start_position + jnp.arange(row_entries, dtype=jnp.int32)
    mode_value = index - harmonic_orders_full // 2
    sample_index = jnp.arange(sidereal_epoch_count, dtype=jnp.int32)
    phase_index = (
        (mode_value % sidereal_epoch_count)[:, None] * sample_index[None, :] % sidereal_epoch_count
    )
    angle = phase_index.astype(jnp.float32) * (2.0 * math.pi / sidereal_epoch_count)
    return (jnp.cos(angle).astype(jnp.bfloat16), jnp.sin(angle).astype(jnp.bfloat16))


def block_of_modes(
    correlator_data_vector,
    start_position,
    row_entries,
    harmonic_orders_full,
    sidereal_epoch_count,
    baseline_list,
    group_extent,
):
    cosine_term, sine_term = twiddles(
        start_position, row_entries, harmonic_orders_full, sidereal_epoch_count
    )
    times_cosine = jnp.dot(
        cosine_term, correlator_data_vector, preferred_element_type=jnp.float32
    ).reshape(row_entries, baseline_list, 2 * group_extent)
    times_sine = jnp.dot(
        sine_term, correlator_data_vector, preferred_element_type=jnp.float32
    ).reshape(row_entries, baseline_list, 2 * group_extent)
    real_part = times_cosine[..., :group_extent] + times_sine[..., group_extent:]
    imag_part = times_cosine[..., group_extent:] - times_sine[..., :group_extent]
    scale = 1.0 / math.sqrt(sidereal_epoch_count)
    return (jnp.concatenate([real_part, imag_part], axis=-1) * scale).astype(jnp.bfloat16)


def harmonics(inverse_rows, mode_rows):
    harm = inverse_rows.shape[2] // 2
    group_extent = mode_rows.shape[2] // 2
    product = jnp.einsum(
        "mbk,mbs->mks", inverse_rows, mode_rows, preferred_element_type=jnp.float32
    )
    real_part = product[:, :harm, :group_extent] - product[:, harm:, group_extent:]
    imag_part = product[:, :harm, group_extent:] + product[:, harm:, :group_extent]
    return jnp.concatenate([real_part, imag_part], axis=-1)


def per_device(visibilities, pseudo_inverse, baseline_group, group_count):
    tm_count = lax.axis_size("tm")
    sidereal_epoch_count = visibilities.shape[0] * tm_count
    harmonic_orders_full = group_count.shape[0] * tm_count
    group_extent = visibilities.shape[2] // 2
    reordered_matrix_lines = lax.all_to_all(
        visibilities, "tm", split_axis=1, concat_axis=0, tiled=True
    )
    local_antenna_pairs = reordered_matrix_lines.shape[1]
    correlator_data_vector = reordered_matrix_lines.reshape(
        sidereal_epoch_count, local_antenna_pairs * 2 * group_extent
    )
    rows_per_block = 128
    start_positions = (
        jnp.arange(harmonic_orders_full // rows_per_block, dtype=jnp.int32) * rows_per_block
    )

    def single_block(start_position):
        return block_of_modes(
            correlator_data_vector,
            start_position,
            rows_per_block,
            harmonic_orders_full,
            sidereal_epoch_count,
            local_antenna_pairs,
            group_extent,
        )

    mode_list = lax.map(single_block, start_positions).reshape(
        harmonic_orders_full, local_antenna_pairs, 2 * group_extent
    )
    local_modes = lax.all_to_all(mode_list, "tm", split_axis=0, concat_axis=1, tiled=True)
    active = (baseline_group[None, :] < group_count[:, None]).astype(jnp.bfloat16)
    masked = pseudo_inverse * active[:, :, None]
    partial_sky = harmonics(masked, local_modes)
    sky = lax.psum_scatter(partial_sky, "base", scatter_dimension=1, tiled=True).astype(
        jnp.bfloat16
    )
    return sky


def solution(mesh):
    in_specs = (P("tm", "base", None), P("tm", "base", None), P("base"), P("tm"))
    out_specs = P("tm", "base", None)
    return jax.shard_map(
        per_device, mesh=mesh, in_specs=in_specs, out_specs=out_specs, check_vma=False
    )
```

profile of v0, /device:TPU:8, one launch (start us, length us, event | category | flops | bytes accessed | tf_op | source)
XLA Modules:
  0.0 313.6 jit_solution(7494910760158446549)
XLA Ops:
  6.5 4.3 %copy.11 = bf16[128,64,128]{2,0,1:T(8,128)(2,1)} copy(bf16[128,64,128]{2,1,0:T(8,128)(2,1)} %param.6) | data formatting | bytes 4194304 | tf_op args[0]
  10.8 14.0 %all-to-all-start = ((bf16[128,64,128]{2,0,1:T(8,128)(2,1)}), bf16[128,64,128]{2,0,1:T(8,128)(2,1)S(1)}, u32[]{:S(2)}, u32[]{:S(2)}) async-start(bf16[128,64,128]{2,0,1:T(8,128)(2,1)} %copy.11), calls=%async_computation | async-start | bytes 4194304 | tf_op jit(solution)/shard_map/all_to_all | solution.py:60
  24.8 50.0 %all-to-all-done = bf16[128,64,128]{2,0,1:T(8,128)(2,1)S(1)} async-done(((bf16[128,64,128]{2,0,1:T(8,128)(2,1)}), bf16[128,64,128]{2,0,1:T(8,128)(2,1)S(1)}, u32[]{:S(2)}, u32[]{:S(2)}) %all-to-all-start) | async-done | bytes 2097184 | tf_op jit(solution)/shard_map/all_to_all | solution.py:60
  74.8 2.2 copy.12
  77.0 1.6 copy.19
  78.6 86.3 %while.12 = (s32[]{:T(128)}, bf16[4,128,2,128]{3,2,1,0:T(2,128)(2,1)}, s32[4]{0:T(128)S(1)}, bf16[4096,256]{1,0:T(8,128)(2,1)}, s32[]{:T(128)}) while((s32[]{:T(128)}, bf16[4,128,2,128]{3,2,1,0:T(2,128)(2,1)}, s32[4]{0:T(128)S(1)}, bf16[4096,256]{1,0:T(8,128)(2,1)}, s32[]{:T(128)}) %tuple.35), condition=%wide.region_1.2_spmd, body=%wide.region_0.1_spmd.sunk | while | flops 552732288 | bytes 5572185 | solution.py:83
  78.6 0.6 dynamic_slice.8
  79.2 0.7 and_select_fusion.2
  79.9 9.4 %fusion.38 = f32[128,256]{1,0:T(8,128)S(1)} fusion(bf16[4096,256]{1,0:T(8,128)(2,1)} %get-tuple-element.115, s32[128]{0:T(128)S(1)} %and_select_fusion.2), kind=kOutput, calls=%fused_computation.11.clone.1 | convolution fusion | flops 276299776 | bytes 2228736 | tf_op jit(solution)/shard_map/while/body/eval_jaxpr/dot_general | solution.py:32
  89.4 0.1 reshape.101
  89.5 9.5 %fusion.37 = f32[128,256]{1,0:T(8,128)S(1)} fusion(bf16[4096,256]{1,0:T(8,128)(2,1)} %get-tuple-element.115, s32[128]{0:T(128)S(1)} %and_select_fusion.2), kind=kOutput, calls=%fused_computation.12.clone.1 | convolution fusion | flops 276299776 | bytes 2228736 | tf_op jit(solution)/shard_map/while/body/eval_jaxpr/dot_general | solution.py:35
  99.0 0.1 reshape.100
  99.1 0.3 fusion.39
  99.4 0.8 fusion.40
  100.2 0.6 dynamic_slice.8
  100.9 0.6 and_select_fusion.2
  101.5 9.4 %fusion.38 = f32[128,256]{1,0:T(8,128)S(1)} fusion(bf16[4096,256]{1,0:T(8,128)(2,1)} %get-tuple-element.115, s32[128]{0:T(128)S(1)} %and_select_fusion.2), kind=kOutput, calls=%fused_computation.11.clone.1 | convolution fusion | flops 276299776 | bytes 2228736 | tf_op jit(solution)/shard_map/while/body/eval_jaxpr/dot_general | solution.py:32
  110.9 0.1 reshape.101
  111.0 9.5 %fusion.37 = f32[128,256]{1,0:T(8,128)S(1)} fusion(bf16[4096,256]{1,0:T(8,128)(2,1)} %get-tuple-element.115, s32[128]{0:T(128)S(1)} %and_select_fusion.2), kind=kOutput, calls=%fused_computation.12.clone.1 | convolution fusion | flops 276299776 | bytes 2228736 | tf_op jit(solution)/shard_map/while/body/eval_jaxpr/dot_general | solution.py:35
  120.5 0.1 reshape.100
  120.6 0.3 fusion.39
  121.0 0.8 fusion.40
  121.8 0.6 dynamic_slice.8
  122.4 0.6 and_select_fusion.2
  123.1 9.4 %fusion.38 = f32[128,256]{1,0:T(8,128)S(1)} fusion(bf16[4096,256]{1,0:T(8,128)(2,1)} %get-tuple-element.115, s32[128]{0:T(128)S(1)} %and_select_fusion.2), kind=kOutput, calls=%fused_computation.11.clone.1 | convolution fusion | flops 276299776 | bytes 2228736 | tf_op jit(solution)/shard_map/while/body/eval_jaxpr/dot_general | solution.py:32
  132.6 9.5 %fusion.37 = f32[128,256]{1,0:T(8,128)S(1)} fusion(bf16[4096,256]{1,0:T(8,128)(2,1)} %get-tuple-element.115, s32[128]{0:T(128)S(1)} %and_select_fusion.2), kind=kOutput, calls=%fused_computation.12.clone.1 | convolution fusion | flops 276299776 | bytes 2228736 | tf_op jit(solution)/shard_map/while/body/eval_jaxpr/dot_general | solution.py:35
  142.1 0.1 reshape.100
  142.2 0.3 fusion.39
  142.5 0.8 fusion.40
  143.4 0.6 dynamic_slice.8
  144.0 0.6 and_select_fusion.2
  144.6 9.4 %fusion.38 = f32[128,256]{1,0:T(8,128)S(1)} fusion(bf16[4096,256]{1,0:T(8,128)(2,1)} %get-tuple-element.115, s32[128]{0:T(128)S(1)} %and_select_fusion.2), kind=kOutput, calls=%fused_computation.11.clone.1 | convolution fusion | flops 276299776 | bytes 2228736 | tf_op jit(solution)/shard_map/while/body/eval_jaxpr/dot_general | solution.py:32
  154.1 0.1 reshape.101
  154.1 9.5 %fusion.37 = f32[128,256]{1,0:T(8,128)S(1)} fusion(bf16[4096,256]{1,0:T(8,128)(2,1)} %get-tuple-element.115, s32[128]{0:T(128)S(1)} %and_select_fusion.2), kind=kOutput, calls=%fused_computation.12.clone.1 | convolution fusion | flops 276299776 | bytes 2228736 | tf_op jit(solution)/shard_map/while/body/eval_jaxpr/dot_general | solution.py:35
  163.7 0.1 reshape.100
  163.7 0.3 fusion.39
  164.1 0.8 fusion.40
  164.9 8.0 %all-to-all-start.1 = ((bf16[512,2,128]{2,1,0:T(2,128)(2,1)}), bf16[512,2,128]{2,1,0:T(2,128)(2,1)S(1)}, u32[]{:S(2)}, u32[]{:S(2)}) async-start(bf16[512,2,128]{2,1,0:T(2,128)(2,1)} %bitcast.5), calls=%async_computation.1 | async-start | bytes 524288 | tf_op jit(solution)/shard_map/all_to_all | solution.py:86
  172.9 0.1 compare_convert_fusion
  173.0 11.1 %all-to-all-done.1 = bf16[512,2,128]{2,1,0:T(2,128)(2,1)S(1)} async-done(((bf16[512,2,128]{2,1,0:T(2,128)(2,1)}), bf16[512,2,128]{2,1,0:T(2,128)(2,1)S(1)}, u32[]{:S(2)}, u32[]{:S(2)}) %all-to-all-start.1) | async-done | bytes 262176 | tf_op jit(solution)/shard_map/all_to_all | solution.py:86
  184.2 0.3 copy.14
  184.5 1.3 fusion.23
  185.8 1.0 slice_subtract_fusion.1
  186.8 2.5 pad_maximum_fusion
  189.3 5.4 %copy.15 = f32[16,512,128]{2,0,1:T(8,128)} copy(f32[16,512,128]{1,2,0:T(8,128)} %pad_maximum_fusion) | data formatting | bytes 8388608 | tf_op jit(solution)/shard_map/concatenate | solution.py:52
  194.8 110.3 %reduce-scatter.2.cloned.1.call-done = f32[16,32,128]{2,0,1:T(8,128)} async-done(((f32[16,512,128]{2,0,1:T(8,128)}), f32[16,32,128]{2,0,1:T(8,128)}) %reduce-scatter.2.cloned.1.call-update) | async-done | bytes 262160 | tf_op jit(solution)/shard_map/reduce_scatter | solution.py:90
  305.1 1.0 convert_element_type.42
  306.1 0.7 copy.16
  (12 shorter events, 0.2 us)
Async XLA Ops:
  10.8 64.0 %all-to-all-start = ((bf16[128,64,128]{2,0,1:T(8,128)(2,1)}), bf16[128,64,128]{2,0,1:T(8,128)(2,1)S(1)}, u32[]{:S(2)}, u32[]{:S(2)}) async-start(bf16[128,64,128]{2,0,1:T(8,128)(2,1)} %copy.11), calls=%async_computation | async-start | bytes 4194304 | tf_op jit(solution)/shard_map/all_to_all | solution.py:60
  78.6 94.3 %copy-start.1 = (s32[64]{0:T(128)S(1)}, s32[64]{0:T(128)}, u32[]{:S(2)}) copy-start(s32[64]{0:T(128)} %param.8) | copy-start | bytes 772
  78.6 94.3 %copy-start.2 = (s32[16]{0:T(128)S(1)}, s32[16]{0:T(128)}, u32[]{:S(2)}) copy-start(s32[16]{0:T(128)} %param.9) | copy-start | bytes 196
  78.6 105.8 %copy-start = (bf16[16,64,1024]{2,1,0:T(8,128)(2,1)S(1)}, bf16[16,64,1024]{2,1,0:T(8,128)(2,1)}, u32[]{:S(2)}) copy-start(bf16[16,64,1024]{2,1,0:T(8,128)(2,1)} %param.7) | copy-start | bytes 6291460
  164.9 19.2 %all-to-all-start.1 = ((bf16[512,2,128]{2,1,0:T(2,128)(2,1)}), bf16[512,2,128]{2,1,0:T(2,128)(2,1)S(1)}, u32[]{:S(2)}, u32[]{:S(2)}) async-start(bf16[512,2,128]{2,1,0:T(2,128)(2,1)} %bitcast.5), calls=%async_computation.1 | async-start | bytes 524288 | tf_op jit(solution)/shard_map/all_to_all | solution.py:86
  172.9 132.2 %reduce-scatter.2.cloned.1.call-start = ((), (), s32[]{:S(2)}) async-start(), calls=%async_computation.3 | async-start | bytes 4456448 | tf_op jit(solution)/shard_map/reduce_scatter | solution.py:90
Sparse Core Ops, SparseCore 0:
  194.9 110.1 reduce-scatter.1
where the time goes:
time: 314 us
  waiting for transfers between devices  171 us (54%)
  matrix products  77.1 us (25%)
  starting transfers between devices  22 us (7%)
  local copies, waits for them, and re-layouts  17.5 us (6%)
  between operations  13.5 us (4%)
  other arithmetic  11.9 us (4%)
    reduce_scatter x1, waiting for transfers between devices, per_device(): lax.psum_scatter(partial_sky, 'base', scatter_dimension=1, tiled=True)  110 us
    all_to_all x1, waiting for transfers between devices, per_device(): lax.all_to_all(visibilities, 'tm', split_axis=1, concat_axis=0, tiled=True)  50 us
    dot_general x4, matrix products, block_of_modes(): jnp.dot(sine_term, correlator_data_vector, preferred_element_type=jnp.flo...  38 us
    dot_general x4, matrix products, block_of_modes(): jnp.dot(cosine_term, correlator_data_vector, preferred_element_type=jnp.f...  37.8 us
    all_to_all x1, starting transfers between devices, per_device(): lax.all_to_all(visibilities, 'tm', split_axis=1, concat_axis=0, tiled=True)  14 us
    all_to_all x1, waiting for transfers between devices, per_device(): lax.all_to_all(mode_list, 'tm', split_axis=0, concat_axis=1, tiled=True)  11.1 us
    all_to_all x1, starting transfers between devices, per_device(): lax.all_to_all(mode_list, 'tm', split_axis=0, concat_axis=1, tiled=True)  7.96 us
  transfers between devices with their start and end apart: 3, of which 3 were waited for; matrix products, arithmetic and copies ran while one was open for 0% of the time, Pallas kernels for 0%

commit v1 on v0

v1 whole, which is shorter than its diff:
```python
import functools
import math

import jax
import jax.numpy as jnp
import ml_dtypes
import numpy as np
from jax import lax
from jax.experimental import pallas as pl
from jax.experimental.pallas import tpu as pltpu
from jax.sharding import Mesh, PartitionSpec as P

MIB = 1 << 20


def tables(modes, samples):
    half = modes // 2
    t = np.arange(samples // 4, dtype=np.int64)
    k = np.arange(half + 1, dtype=np.int64)[:, None] * t[None, :] % samples
    angle = np.arange(samples, dtype=np.float64) * (2.0 * math.pi / samples)
    cosine = np.cos(angle).astype(np.float32).astype(ml_dtypes.bfloat16)[k]
    sine = np.sin(angle).astype(np.float32).astype(ml_dtypes.bfloat16)[k]
    rest = np.zeros((14, samples // 4), ml_dtypes.bfloat16)
    return np.concatenate([cosine[:half], sine[:half], cosine[half:], sine[half:], rest])


def permutation(order):
    matrix = np.zeros((len(order), len(order)), ml_dtypes.bfloat16)
    matrix[np.arange(len(order)), order] = 1
    return matrix


def whole():
    return pl.BlockSpec(memory_space=pltpu.VMEM)


def by_baseline(visibilities):
    times, baselines, width = visibilities.shape
    half, tile, block = baselines // 2, 16, 32
    blocks = times // block

    def kernel(in_ref, out_ref, near, turned, in_sems, out_sems):
        def fetch(i):
            at = pl.ds(i * block, block)
            return pltpu.make_async_copy(in_ref.at[at], near.at[at], in_sems.at[i])

        def store(i):
            at = pl.ds(i * block, block)
            return pltpu.make_async_copy(
                turned.at[:, at, :], out_ref.at[:, at, :], out_sems.at[i]
            )

        for i in range(blocks):
            fetch(i).start()
        for i in range(blocks):
            fetch(i).wait()
            for t in range(i * block, (i + 1) * block, tile):
                for b in range(0, baselines, tile):
                    rows = jnp.swapaxes(near[t : t + tile, b : b + tile, :], 0, 1)
                    h, d = divmod(b, half)
                    turned[d : d + tile, t : t + tile, h * width : (h + 1) * width] = rows
            store(i).start()
        for i in range(blocks):
            store(i).wait()

    out = (half, times, 2 * width)
    return pl.pallas_call(
        kernel,
        in_specs=[pl.BlockSpec(memory_space=pl.ANY)],
        out_specs=pl.BlockSpec(memory_space=pl.ANY),
        out_shape=jax.ShapeDtypeStruct(out, jnp.bfloat16),
        scratch_shapes=[
            pltpu.VMEM(visibilities.shape, jnp.bfloat16),
            pltpu.VMEM(out, jnp.bfloat16),
            pltpu.SemaphoreType.DMA((blocks,)),
            pltpu.SemaphoreType.DMA((blocks,)),
        ],
        compiler_params=pltpu.CompilerParams(vmem_limit_bytes=56 * MIB),
        cost_estimate=pl.CostEstimate(
            flops=0, bytes_accessed=4 * visibilities.size, transcendentals=0
        ),
        name="by_baseline",
    )(visibilities)


def prepare(blocks):
    each_m, baselines, width = blocks[0].shape
    harm, peers = width // 2, len(blocks)
    depth = 2 * peers * baselines

    def kernel(*refs):
        block_refs, inverse_ref = refs[:peers], refs[peers]
        for m in range(each_m):
            for part in range(2):
                at = slice(part * harm, (part + 1) * harm)
                for p in range(0, peers, 2):
                    two = [block_refs[p + i][m, :, at] for i in range(2)]
                    to = (part * peers + p) * baselines
                    inverse_ref[m, :, to : to + 2 * baselines] = jnp.concatenate(two, axis=0).T

    return pl.pallas_call(
        kernel,
        in_specs=[whole()] * peers,
        out_specs=whole(),
        out_shape=pltpu.VMEM((each_m, harm, depth), jnp.bfloat16),
        compiler_params=pltpu.CompilerParams(vmem_limit_bytes=12 * MIB),
        cost_estimate=pl.CostEstimate(
            flops=0, bytes_accessed=4 * each_m * harm * depth, transcendentals=0
        ),
        name="prepare",
    )(*blocks)


def transform(data, modes, ns):
    samples, width = data.shape
    quarter, half = samples // 4, modes // 2
    scale = 1.0 / math.sqrt(samples)
    table = tables(modes, samples)

    def turn(v):
        parts = []
        for b in range(0, width, 2 * ns):
            parts += [v[:, b + ns : b + 2 * ns], -v[:, b : b + ns]]
        return jnp.concatenate(parts, axis=1)

    def kernel(table_ref, data_ref, out_ref):
        z = [
            jnp.dot(
                table_ref[...],
                data_ref[j * quarter : (j + 1) * quarter, :],
                preferred_element_type=jnp.float32,
            )
            for j in range(4)
        ]
        c = [v[:half] for v in z]
        s = [v[half : 2 * half] for v in z]
        row = lax.broadcasted_iota(jnp.int32, (half, width), 0)
        odd = row % 2 == 1
        sign = jnp.where(odd, -1.0, 1.0)
        late = jnp.where(row % 4 >= 2, -1.0, 1.0)
        p_c, p_s = c[1] + sign * c[3], s[1] + sign * s[3]
        u = c[0] + sign * c[2] + late * jnp.where(odd, -p_s, p_c)
        v = turn(s[0] + sign * s[2] + late * jnp.where(odd, p_c, p_s))
        plus, minus = (u + v) * scale, (u - v) * scale
        last = z[0][2 * half :] + z[1][2 * half :] + z[2][2 * half :] + z[3][2 * half :]
        last = (last[0:1] - turn(last[1:2])) * scale
        minus = jnp.where(row == 0, last, minus).astype(jnp.bfloat16)
        both = sum(lax.broadcasted_iota(jnp.int32, (half, half), d) for d in (0, 1))
        back = jnp.where(both % half == 0, 1.0, 0.0).astype(jnp.bfloat16)
        out_ref[:half, :] = jnp.dot(
            back, minus, preferred_element_type=jnp.float32
        ).astype(jnp.bfloat16)
        out_ref[half:, :] = plus.astype(jnp.bfloat16)

    return pl.pallas_call(
        kernel,
        in_specs=[whole()] * 2,
        out_specs=whole(),
        out_shape=jax.ShapeDtypeStruct((modes, width), jnp.bfloat16),
        compiler_params=pltpu.CompilerParams(vmem_limit_bytes=12 * MIB),
        cost_estimate=pl.CostEstimate(
            flops=2 * table.size * 4 * width,
            bytes_accessed=2 * table.size + 2 * data.size,
            transcendentals=0,
        ),
        name="transform",
    )(table, data)


def product(inverse, rows, sources, devices, ns):
    each_m, harm, _ = inverse.shape
    n_rows, width = rows.shape
    peers = sources.shape[0]
    outer = n_rows // (each_m * peers)
    order = np.arange(n_rows).reshape(outer, peers, each_m).transpose(2, 1, 0).reshape(-1)
    per = harm // devices

    def kernel(sources_ref, turn_ref, rows_ref, inverse_ref, out_ref, sorted_rows):
        sorted_rows[...] = jnp.dot(
            turn_ref[...], rows_ref[...], preferred_element_type=jnp.float32
        )
        for m in range(each_m):
            plain, turned = [], []
            for p in range(peers):
                at = pl.multiple_of((m * peers + sources_ref[p]) * outer, outer)
                for h in range(0, width, 2 * ns):
                    one = sorted_rows[pl.ds(at, outer), h : h + 2 * ns]
                    plain.append(one)
                    turned.append(jnp.concatenate([-one[:, ns:], one[:, :ns]], axis=1))
            weights = jnp.concatenate(plain + turned, axis=0).astype(jnp.bfloat16)
            sky = jnp.dot(inverse_ref[m], weights, preferred_element_type=jnp.float32)
            out_ref[:, m] = sky.astype(jnp.bfloat16).reshape(devices, per, 2 * ns)

    return pl.pallas_call(
        kernel,
        in_specs=[
            pl.BlockSpec(memory_space=pltpu.SMEM),
            whole(),
            whole(),
            whole(),
        ],
        out_specs=whole(),
        out_shape=jax.ShapeDtypeStruct((devices, each_m, per, 2 * ns), jnp.bfloat16),
        scratch_shapes=[
            pltpu.VMEM((n_rows, width), jnp.float32),
        ],
        compiler_params=pltpu.CompilerParams(vmem_limit_bytes=12 * MIB),
        cost_estimate=pl.CostEstimate(
            flops=4 * inverse.size * ns, bytes_accessed=2 * inverse.size, transcendentals=0
        ),
        name="product",
    )(sources, permutation(order), rows, inverse)


def per_device(visibilities, pseudo_inverse, baseline_group, group_count):
    tm, nx, nh, nc = (lax.axis_size(a) for a in ("tm", "x", "h", "c"))
    peers = nx * nc
    x, c = lax.axis_index("x"), lax.axis_index("c")
    local_t, local_b, width = visibilities.shape
    samples = local_t * tm
    mine_m = group_count.shape[0]
    modes = mine_m * tm
    each_m = mine_m // peers
    ns = width // 2

    data = by_baseline(visibilities)
    data = lax.all_to_all(data, "tm", split_axis=0, concat_axis=0, tiled=True)
    data = data.reshape(samples, 2 * width)

    active = (baseline_group[None, :] < group_count[:, None]).astype(jnp.bfloat16)
    masked = pseudo_inverse * active[:, :, None]
    blocks, sources = [], []
    for dx in range(nx):
        for dc in range(nc):
            to = (x + dx) % nx * nc + (c + dc) % nc
            block = lax.dynamic_slice_in_dim(masked, to * each_m, each_m, 0)
            if dx or dc:
                moves = [
                    (i, (i // nc + dx) % nx * nc + (i % nc + dc) % nc) for i in range(peers)
                ]
                block = lax.ppermute(block, ("x", "c"), moves)
            blocks.append(block)
            sources.append((x - dx) % nx * nc + (c - dc) % nc)
    inverse, data = lax.optimization_barrier((prepare(blocks), data))
    rows = transform(data, modes, ns)

    rows = lax.all_to_all(rows, ("tm", "x", "c"), split_axis=0, concat_axis=0, tiled=True)
    sky = product(inverse, rows, jnp.stack(sources), nx * nh * nc, ns)

    sky = lax.all_to_all(sky, ("x", "h", "c"), split_axis=0, concat_axis=0, tiled=True)
    sky = sky.reshape(nx, nh, nc, each_m, -1, width).astype(jnp.float32).sum(axis=1)
    return sky.reshape(mine_m, -1, width).astype(jnp.bfloat16)


def solution(mesh):
    tm, base = mesh.devices.shape
    fine = Mesh(mesh.devices.reshape(tm, base // 4, 2, 2), ("tm", "x", "h", "c"))
    b = ("x", "h", "c")
    in_specs = (P("tm", b, None), P("tm", b, None), P(b), P("tm"))
    return jax.shard_map(
        per_device, mesh=fine, in_specs=in_specs, out_specs=P("tm", b, None), check_vma=False
    )
```

time: 314 us -> 127 us (0.40)
  waiting for transfers between devices: 171 us -> 34.2 us
  matrix products: 77.1 us -> 0 us
  starting transfers between devices: 22 us -> 56.3 us
  blocking collectives: 0 us -> 23.5 us
  local copies, waits for them, and re-layouts: 17.5 us -> 2.44 us
  between operations: 13.5 us -> 0.39 us
  other arithmetic: 11.9 us -> 0.98 us
  Pallas kernels: 0 us -> 8.19 us
    reduce_scatter x1 -> x0, waiting for transfers between devices: 110 us -> none  [per_device(): lax.psum_scatter(partial_sky, 'base', scatter_dimension=1, tiled=True)]
    dot_general x9 -> x0, matrix products: 77.1 us -> none  [the longest x4 38 us: block_of_modes(): jnp.dot(sine_term, correlator_data_vector, preferred_element_type=jnp.flo...]
    all_to_all x2, waiting for transfers between devices: 61.2 us -> 27.9 us  [the longest x1 14.4 us: per_device(): lax.all_to_all(rows, ('tm', 'x', 'c'), split_axis=0, concat_axis=0, tiled...]
    ppermute x0 -> x7, starting transfers between devices: none -> 29 us  [per_device(): block = lax.ppermute(block, ('x', 'c'), moves)]
    all_to_all x0 -> x1, blocking collectives: none -> 23.5 us  [per_device(): lax.all_to_all(sky, ('x', 'h', 'c'), split_axis=0, concat_axis=0, tiled=T...]
    pallas_call x0 -> x4, Pallas kernels: none -> 8.19 us  [the longest x1 3.31 us: transform(): pl.pallas_call(kernel, in_specs=[whole()] * 2, out_specs=whole(), out_sha...]
    ppermute x0 -> x7, waiting for transfers between devices: none -> 6.32 us  [per_device(): block = lax.ppermute(block, ('x', 'c'), moves)]
    concatenate x1 -> x0, local copies, waits for them, and re-layouts: 5.45 us -> none  [harmonics(): return jnp.concatenate([real_part, imag_part], axis=-1)]
  transfers between devices with their start and end apart: 3 -> 9, of which waited for: 3 -> 4; matrix products, arithmetic and copies ran while one was open for 0% -> 0% of each run, Pallas kernels for 0% -> 1%
where the time goes in v1:
time: 127 us; the launch traced here: 126 us
  starting transfers between devices  56.3 us (44%)
  waiting for transfers between devices  34.2 us (27%)
  blocking collectives  23.5 us (19%)
  Pallas kernels  8.19 us (6%)
  local copies, waits for them, and re-layouts  2.44 us (2%)
    ppermute x7, starting transfers between devices, per_device(): block = lax.ppermute(block, ('x', 'c'), moves)  29 us
    all_to_all x1, blocking collectives, per_device(): lax.all_to_all(sky, ('x', 'h', 'c'), split_axis=0, concat_axis=0, tiled=T...  23.5 us
    all_to_all x1, waiting for transfers between devices, per_device(): lax.all_to_all(rows, ('tm', 'x', 'c'), split_axis=0, concat_axis=0, tiled...  14.4 us
    all_to_all x1, starting transfers between devices, per_device(): data = lax.all_to_all(data, 'tm', split_axis=0, concat_axis=0, tiled=True)  14.2 us
    all_to_all x1, waiting for transfers between devices, per_device(): data = lax.all_to_all(data, 'tm', split_axis=0, concat_axis=0, tiled=True)  13.4 us
    all_to_all x1, starting transfers between devices, per_device(): lax.all_to_all(rows, ('tm', 'x', 'c'), split_axis=0, concat_axis=0, tiled...  13.1 us
    ppermute x7, waiting for transfers between devices, per_device(): block = lax.ppermute(block, ('x', 'c'), moves)  6.32 us
    pallas_call x1, Pallas kernels, transform(): pl.pallas_call(kernel, in_specs=[whole()] * 2, out_specs=whole(), out_sha...  3.31 us
  transfers between devices with their start and end apart: 9, of which 4 were waited for; matrix products, arithmetic and copies ran while one was open for 0% of the time, Pallas kernels for 1%

profile of v1, /device:TPU:8, one launch (start us, length us, event | category | flops | bytes accessed | tf_op | source)
XLA Modules:
  0.0 126.0 jit_solution(64334102541081454)
XLA Ops:
  0.0 2.6 %by_baseline.1 = bf16[32,128,256]{2,1,0:T(8,128)(2,1)} custom-call(bf16[128,64,128]{2,1,0:T(8,128)(2,1)} %in_ref.1), custom_call_target="tpu_custom_call" | custom-call | bytes 4194304 | tf_op jit(solution)/shard_map/by_baseline/pallas_call | solution.py:67
  2.6 0.0 copy-start.3
  2.7 0.0 copy-start.4
  2.7 0.0 copy-start.2
  2.7 14.2 %all-to-all-start = ((bf16[32,128,256]{2,1,0:T(8,128)(2,1)}), bf16[32,128,256]{2,1,0:T(8,128)(2,1)}, u32[]{:S(2)}, u32[]{:S(2)}) async-start(bf16[32,128,256]{2,1,0:T(8,128)(2,1)} %by_baseline.1), calls=%async_computation | async-start | bytes 4194304 | tf_op jit(solution)/shard_map/all_to_all | solution.py:227
  17.0 0.0 copy-done.3
  17.0 0.0 copy-done.4
  17.0 0.1 compare_convert_fusion
  17.0 0.0 copy-done.2
  17.0 0.2 broadcast_multiply_fusion
  17.3 0.2 constant_dynamic-slice_fusion
  17.5 3.5 %collective-permute-start.6 = (bf16[2,64,1024]{2,1,0:T(8,128)(2,1)S(1)}, bf16[2,64,1024]{2,1,0:T(8,128)(2,1)S(1)}, u32[]{:S(2)}, u32[]{:S(2)}) collective-permute-start(bf16[2,64,1024]{2,1,0:T(8,128)(2,1)S(1)} %get-tuple-element.9), channel_id=1, source_target_pairs={{0,13},{1,12},{4,1},{5,0},{8,5},{9,4},{12,9},{13,8},{2,15},{3,14},... | collective-permute-start | bytes 786440 | tf_op jit(solution)/shard_map/ppermute | solution.py:241
  21.0 3.0 %collective-permute-start.5 = (bf16[2,64,1024]{2,1,0:T(8,128)(2,1)S(1)}, bf16[2,64,1024]{2,1,0:T(8,128)(2,1)S(1)}, u32[]{:S(2)}, u32[]{:S(2)}) collective-permute-start(bf16[2,64,1024]{2,1,0:T(8,128)(2,1)S(1)} %get-tuple-element.10), channel_id=1, source_target_pairs={{0,12},{1,13},{4,0},{5,1},{8,4},{9,5},{12,8},{13,9},{2,14},{3,15},... | collective-permute-start | bytes 786440 | tf_op jit(solution)/shard_map/ppermute | solution.py:241
  24.1 2.7 %collective-permute-start.4 = (bf16[2,64,1024]{2,1,0:T(8,128)(2,1)S(1)}, bf16[2,64,1024]{2,1,0:T(8,128)(2,1)S(1)}, u32[]{:S(2)}, u32[]{:S(2)}) collective-permute-start(bf16[2,64,1024]{2,1,0:T(8,128)(2,1)S(1)} %get-tuple-element.11), channel_id=1, source_target_pairs={{0,9},{1,8},{4,13},{5,12},{8,1},{9,0},{12,5},{13,4},{2,11},{3,10},... | collective-permute-start | bytes 786440 | tf_op jit(solution)/shard_map/ppermute | solution.py:241
  26.7 4.9 %collective-permute-start.3 = (bf16[2,64,1024]{2,1,0:T(8,128)(2,1)S(1)}, bf16[2,64,1024]{2,1,0:T(8,128)(2,1)S(1)}, u32[]{:S(2)}, u32[]{:S(2)}) collective-permute-start(bf16[2,64,1024]{2,1,0:T(8,128)(2,1)S(1)} %get-tuple-element.12), channel_id=1, source_target_pairs={{0,8},{1,9},{4,12},{5,13},{8,0},{9,1},{12,4},{13,5},{2,10},{3,11},... | collective-permute-start | bytes 786440 | tf_op jit(solution)/shard_map/ppermute | solution.py:241
  31.7 2.0 %collective-permute-start.2 = (bf16[2,64,1024]{2,1,0:T(8,128)(2,1)S(1)}, bf16[2,64,1024]{2,1,0:T(8,128)(2,1)S(1)}, u32[]{:S(2)}, u32[]{:S(2)}) collective-permute-start(bf16[2,64,1024]{2,1,0:T(8,128)(2,1)S(1)} %get-tuple-element.13), channel_id=1, source_target_pairs={{0,5},{1,4},{4,9},{5,8},{8,13},{9,12},{12,1},{13,0},{2,7},{3,6},{6... | collective-permute-start | bytes 786440 | tf_op jit(solution)/shard_map/ppermute | solution.py:241
  33.7 0.0 collective-permute-done.6.refs_7_
  33.7 3.0 %collective-permute-start.1 = (bf16[2,64,1024]{2,1,0:T(8,128)(2,1)S(1)}, bf16[2,64,1024]{2,1,0:T(8,128)(2,1)S(1)}, u32[]{:S(2)}, u32[]{:S(2)}) collective-permute-start(bf16[2,64,1024]{2,1,0:T(8,128)(2,1)S(1)} %get-tuple-element.14), channel_id=1, source_target_pairs={{0,4},{1,5},{4,8},{5,9},{8,12},{9,13},{12,0},{13,1},{2,6},{3,7},{6... | collective-permute-start | bytes 786440 | tf_op jit(solution)/shard_map/ppermute | solution.py:241
  36.7 0.0 collective-permute-done.5.refs_6_
  36.7 9.8 %collective-permute-start = (bf16[2,64,1024]{2,1,0:T(8,128)(2,1)S(1)}, bf16[2,64,1024]{2,1,0:T(8,128)(2,1)S(1)}, u32[]{:S(2)}, u32[]{:S(2)}) collective-permute-start(bf16[2,64,1024]{2,1,0:T(8,128)(2,1)S(1)} %get-tuple-element.15), channel_id=1, source_target_pairs={{0,1},{1,0},{4,5},{5,4},{8,9},{9,8},{12,13},{13,12},{2,3},{3,2},{6... | collective-permute-start | bytes 786440 | tf_op jit(solution)/shard_map/ppermute | solution.py:241
  46.6 0.0 collective-permute-done.4.refs_5_
  46.6 0.0 collective-permute-done.3.refs_4_
  46.6 0.7 collective-permute-done.2.refs_3_
  47.3 5.6 %collective-permute-done.1.refs_2_ = bf16[2,64,1024]{2,1,0:T(8,128)(2,1)S(1)} collective-permute-done((bf16[2,64,1024]{2,1,0:T(8,128)(2,1)S(1)}, bf16[2,64,1024]{2,1,0:T(8,128)(2,1)S(1)}, u32[]{:S(2)}, u32[]{:S(2)}) %collective-permute-start.1) | collective-permute-done | bytes 262176 | tf_op jit(solution)/shard_map/ppermute | solution.py:241
  52.9 0.0 collective-permute-done.refs_1_
  52.9 0.7 prepare.1.inverse_ref
  53.6 13.4 %all-to-all-done = bf16[32,128,256]{2,1,0:T(8,128)(2,1)} async-done(((bf16[32,128,256]{2,1,0:T(8,128)(2,1)}), bf16[32,128,256]{2,1,0:T(8,128)(2,1)}, u32[]{:S(2)}, u32[]{:S(2)}) %all-to-all-start) | async-done | bytes 2097184 | tf_op jit(solution)/shard_map/all_to_all | solution.py:227
  67.0 0.0 copy-start.1
  67.0 1.2 copy-done.1
  68.3 0.0 copy-start
  68.3 3.3 %transform.1 = bf16[512,256]{1,0:T(8,128)(2,1)S(1)} custom-call(bf16[528,1024]{1,0:T(8,128)(2,1)S(1)} %copy-done.1, bf16[4096,256]{1,0:T(8,128)(2,1)} %bitcast.8.data_ref), custom_call_target="tpu_custom_call" | custom-call | flops 1107296256 | bytes 3178496 | tf_op jit(solution)/shard_map/transform/pallas_call | solution.py:155
  71.6 0.8 all_to_all.14
  72.4 13.1 %all-to-all-start.1 = ((bf16[256,2,256]{2,1,0:T(2,128)(2,1)}), bf16[256,2,256]{2,1,0:T(2,128)(2,1)S(1)}, u32[]{:S(2)}, u32[]{:S(2)}) async-start(bf16[256,2,256]{2,1,0:T(2,128)(2,1)} %all_to_all.14), calls=%async_computation.1 | async-start | bytes 524288 | tf_op jit(solution)/shard_map/all_to_all | solution.py:247
  85.6 0.1 stack.35.sources_ref
  85.7 14.4 %all-to-all-done.1 = bf16[256,2,256]{2,1,0:T(2,128)(2,1)S(1)} async-done(((bf16[256,2,256]{2,1,0:T(2,128)(2,1)}), bf16[256,2,256]{2,1,0:T(2,128)(2,1)S(1)}, u32[]{:S(2)}, u32[]{:S(2)}) %all-to-all-start.1) | async-done | bytes 262176 | tf_op jit(solution)/shard_map/all_to_all | solution.py:247
  100.1 0.1 all_to_all.16.rows_ref
  100.2 0.0 copy-done
  100.2 1.6 %product.1 = bf16[16,2,32,128]{3,2,1,0:T(8,128)(2,1)S(1)} custom-call(s32[8]{0:T(128)S(1)} %stack.35.sources_ref, bf16[512,512]{1,0:T(8,128)(2,1)S(1)} %copy-done, bf16[512,256]{1,0:T(8,128)(2,1)S(1)} %all_to_all.16.rows_ref, bf16[2,512,1024]{2,1,0:T(8,128)(2,1)S(1)} %prepare.1.inverse_ref), custom_call_target="tpu_custom_call" | custom-call | flops 268435456 | bytes 2097152 | tf_op jit(solution)/shard_map/product/pallas_call | solution.py:194
  101.7 23.5 %all_to_all.21 = bf16[16,2,32,128]{3,2,1,0:T(8,128)(2,1)S(1)} all-to-all(bf16[16,2,32,128]{3,2,1,0:T(8,128)(2,1)S(1)} %product.1), channel_id=1, replica_groups=mesh['tm'=32,'x'=4,'h'=2,'c'=2] {'x','h','c'}, dimensions={0} | all-to-all | bytes 524288 | tf_op jit(solution)/shard_map/all_to_all | solution.py:250
  125.3 0.7 reduce
Async XLA Ops:
  2.6 14.3 %copy-start.3 = (s32[64]{0:T(128)S(1)}, s32[64]{0:T(128)}, u32[]{:S(2)}) copy-start(s32[64]{0:T(128)} %param.8) | copy-start | bytes 772
  2.7 14.3 %copy-start.4 = (s32[16]{0:T(128)S(1)}, s32[16]{0:T(128)}, u32[]{:S(2)}) copy-start(s32[16]{0:T(128)} %param.9) | copy-start | bytes 196
  2.7 14.4 %copy-start.2 = (bf16[16,64,1024]{2,1,0:T(8,128)(2,1)S(1)}, bf16[16,64,1024]{2,1,0:T(8,128)(2,1)}, u32[]{:S(2)}) copy-start(bf16[16,64,1024]{2,1,0:T(8,128)(2,1)} %param.7) | copy-start | bytes 6291460
  2.7 64.3 %all-to-all-start = ((bf16[32,128,256]{2,1,0:T(8,128)(2,1)}), bf16[32,128,256]{2,1,0:T(8,128)(2,1)}, u32[]{:S(2)}, u32[]{:S(2)}) async-start(bf16[32,128,256]{2,1,0:T(8,128)(2,1)} %by_baseline.1), calls=%async_computation | async-start | bytes 4194304 | tf_op jit(solution)/shard_map/all_to_all | solution.py:227
  17.5 16.2 %collective-permute-start.6 = (bf16[2,64,1024]{2,1,0:T(8,128)(2,1)S(1)}, bf16[2,64,1024]{2,1,0:T(8,128)(2,1)S(1)}, u32[]{:S(2)}, u32[]{:S(2)}) collective-permute-start(bf16[2,64,1024]{2,1,0:T(8,128)(2,1)S(1)} %get-tuple-element.9), channel_id=1, source_target_pairs={{0,13},{1,12},{4,1},{5,0},{8,5},{9,4},{12,9},{13,8},{2,15},{3,14},... | collective-permute-start | bytes 786440 | tf_op jit(solution)/shard_map/ppermute | solution.py:241
  21.0 15.7 %collective-permute-start.5 = (bf16[2,64,1024]{2,1,0:T(8,128)(2,1)S(1)}, bf16[2,64,1024]{2,1,0:T(8,128)(2,1)S(1)}, u32[]{:S(2)}, u32[]{:S(2)}) collective-permute-start(bf16[2,64,1024]{2,1,0:T(8,128)(2,1)S(1)} %get-tuple-element.10), channel_id=1, source_target_pairs={{0,12},{1,13},{4,0},{5,1},{8,4},{9,5},{12,8},{13,9},{2,14},{3,15},... | collective-permute-start | bytes 786440 | tf_op jit(solution)/shard_map/ppermute | solution.py:241
  24.1 22.5 %collective-permute-start.4 = (bf16[2,64,1024]{2,1,0:T(8,128)(2,1)S(1)}, bf16[2,64,1024]{2,1,0:T(8,128)(2,1)S(1)}, u32[]{:S(2)}, u32[]{:S(2)}) collective-permute-start(bf16[2,64,1024]{2,1,0:T(8,128)(2,1)S(1)} %get-tuple-element.11), channel_id=1, source_target_pairs={{0,9},{1,8},{4,13},{5,12},{8,1},{9,0},{12,5},{13,4},{2,11},{3,10},... | collective-permute-start | bytes 786440 | tf_op jit(solution)/shard_map/ppermute | solution.py:241
  26.7 19.8 %collective-permute-start.3 = (bf16[2,64,1024]{2,1,0:T(8,128)(2,1)S(1)}, bf16[2,64,1024]{2,1,0:T(8,128)(2,1)S(1)}, u32[]{:S(2)}, u32[]{:S(2)}) collective-permute-start(bf16[2,64,1024]{2,1,0:T(8,128)(2,1)S(1)} %get-tuple-element.12), channel_id=1, source_target_pairs={{0,8},{1,9},{4,12},{5,13},{8,0},{9,1},{12,4},{13,5},{2,10},{3,11},... | collective-permute-start | bytes 786440 | tf_op jit(solution)/shard_map/ppermute | solution.py:241
  31.7 15.6 %collective-permute-start.2 = (bf16[2,64,1024]{2,1,0:T(8,128)(2,1)S(1)}, bf16[2,64,1024]{2,1,0:T(8,128)(2,1)S(1)}, u32[]{:S(2)}, u32[]{:S(2)}) collective-permute-start(bf16[2,64,1024]{2,1,0:T(8,128)(2,1)S(1)} %get-tuple-element.13), channel_id=1, source_target_pairs={{0,5},{1,4},{4,9},{5,8},{8,13},{9,12},{12,1},{13,0},{2,7},{3,6},{6... | collective-permute-start | bytes 786440 | tf_op jit(solution)/shard_map/ppermute | solution.py:241
  33.7 19.2 %collective-permute-start.1 = (bf16[2,64,1024]{2,1,0:T(8,128)(2,1)S(1)}, bf16[2,64,1024]{2,1,0:T(8,128)(2,1)S(1)}, u32[]{:S(2)}, u32[]{:S(2)}) collective-permute-start(bf16[2,64,1024]{2,1,0:T(8,128)(2,1)S(1)} %get-tuple-element.14), channel_id=1, source_target_pairs={{0,4},{1,5},{4,8},{5,9},{8,12},{9,13},{12,0},{13,1},{2,6},{3,7},{6... | collective-permute-start | bytes 786440 | tf_op jit(solution)/shard_map/ppermute | solution.py:241
  36.7 16.2 %collective-permute-start = (bf16[2,64,1024]{2,1,0:T(8,128)(2,1)S(1)}, bf16[2,64,1024]{2,1,0:T(8,128)(2,1)S(1)}, u32[]{:S(2)}, u32[]{:S(2)}) collective-permute-start(bf16[2,64,1024]{2,1,0:T(8,128)(2,1)S(1)} %get-tuple-element.15), channel_id=1, source_target_pairs={{0,1},{1,0},{4,5},{5,4},{8,9},{9,8},{12,13},{13,12},{2,3},{3,2},{6... | collective-permute-start | bytes 786440 | tf_op jit(solution)/shard_map/ppermute | solution.py:241
  67.0 1.2 copy-start.1
  68.3 31.9 %copy-start = (bf16[512,512]{1,0:T(8,128)(2,1)S(1)}, bf16[512,512]{1,0:T(8,128)(2,1)}, u32[]{:S(2)}) copy-start(bf16[512,512]{1,0:T(8,128)(2,1)} %constant.127.clone.turn_ref) | copy-start | bytes 1572868
  72.4 27.7 %all-to-all-start.1 = ((bf16[256,2,256]{2,1,0:T(2,128)(2,1)}), bf16[256,2,256]{2,1,0:T(2,128)(2,1)S(1)}, u32[]{:S(2)}, u32[]{:S(2)}) async-start(bf16[256,2,256]{2,1,0:T(2,128)(2,1)} %all_to_all.14), calls=%async_computation.1 | async-start | bytes 524288 | tf_op jit(solution)/shard_map/all_to_all | solution.py:247

commit v2 on v1

--- a/solution.py
+++ b/solution.py
@@ -22,12 +22,6 @@
     sine = np.sin(angle).astype(np.float32).astype(ml_dtypes.bfloat16)[k]
     rest = np.zeros((14, samples // 4), ml_dtypes.bfloat16)
     return np.concatenate([cosine[:half], sine[:half], cosine[half:], sine[half:], rest])
-
-
-def permutation(order):
-    matrix = np.zeros((len(order), len(order)), ml_dtypes.bfloat16)
-    matrix[np.arange(len(order)), order] = 1
-    return matrix
 
 
 def whole():
@@ -83,13 +77,13 @@
     )(visibilities)
 
 
-def prepare(blocks):
+def prepare(blocks, after):
     each_m, baselines, width = blocks[0].shape
     harm, peers = width // 2, len(blocks)
     depth = 2 * peers * baselines
 
     def kernel(*refs):
-        block_refs, inverse_ref = refs[:peers], refs[peers]
+        block_refs, inverse_ref = refs[:peers], refs[peers + 1]
         for m in range(each_m):
             for part in range(2):
                 at = slice(part * harm, (part + 1) * harm)
@@ -100,15 +94,15 @@
 
     return pl.pallas_call(
         kernel,
-        in_specs=[whole()] * peers,
+        in_specs=[whole()] * peers + [pl.BlockSpec(memory_space=pl.ANY)],
         out_specs=whole(),
         out_shape=pltpu.VMEM((each_m, harm, depth), jnp.bfloat16),
-        compiler_params=pltpu.CompilerParams(vmem_limit_bytes=12 * MIB),
+        compiler_params=pltpu.CompilerParams(vmem_limit_bytes=56 * MIB),
         cost_estimate=pl.CostEstimate(
             flops=0, bytes_accessed=4 * each_m * harm * depth, transcendentals=0
         ),
         name="prepare",
-    )(*blocks)
+    )(*blocks, after)
 
 
 def transform(data, modes, ns):
@@ -172,13 +166,16 @@
     n_rows, width = rows.shape
     peers = sources.shape[0]
     outer = n_rows // (each_m * peers)
-    order = np.arange(n_rows).reshape(outer, peers, each_m).transpose(2, 1, 0).reshape(-1)
+    bits = [n.bit_length() - 1 for n in (outer, peers)]
     per = harm // devices
 
-    def kernel(sources_ref, turn_ref, rows_ref, inverse_ref, out_ref, sorted_rows):
-        sorted_rows[...] = jnp.dot(
-            turn_ref[...], rows_ref[...], preferred_element_type=jnp.float32
-        )
+    def kernel(sources_ref, rows_ref, inverse_ref, out_ref, sorted_rows):
+        to = lax.broadcasted_iota(jnp.int32, (n_rows, 1), 0)
+        o, p, m = to & (outer - 1), (to >> bits[0]) & (peers - 1), to >> (bits[0] + bits[1])
+        source = (o * peers + p) * each_m + m
+        column = lax.broadcasted_iota(jnp.int32, (n_rows, n_rows), 1)
+        matrix = jnp.where(column == source, 1.0, 0.0).astype(jnp.bfloat16)
+        sorted_rows[...] = jnp.dot(matrix, rows_ref[...], preferred_element_type=jnp.float32)
         for m in range(each_m):
             plain, turned = [], []
             for p in range(peers):
@@ -197,7 +194,6 @@
             pl.BlockSpec(memory_space=pltpu.SMEM),
             whole(),
             whole(),
-            whole(),
         ],
         out_specs=whole(),
         out_shape=jax.ShapeDtypeStruct((devices, each_m, per, 2 * ns), jnp.bfloat16),
@@ -209,7 +205,7 @@
             flops=4 * inverse.size * ns, bytes_accessed=2 * inverse.size, transcendentals=0
         ),
         name="product",
-    )(sources, permutation(order), rows, inverse)
+    )(sources, rows, inverse)
 
 
 def per_device(visibilities, pseudo_inverse, baseline_group, group_count):
@@ -241,8 +237,9 @@
                 block = lax.ppermute(block, ("x", "c"), moves)
             blocks.append(block)
             sources.append((x - dx) % nx * nc + (c - dc) % nc)
-    inverse, data = lax.optimization_barrier((prepare(blocks), data))
+    data, *blocks = lax.optimization_barrier((data, *blocks))
     rows = transform(data, modes, ns)
+    inverse = prepare(blocks, rows)
 
     rows = lax.all_to_all(rows, ("tm", "x", "c"), split_axis=0, concat_axis=0, tiled=True)
     sky = product(inverse, rows, jnp.stack(sources), nx * nh * nc, ns)

time: 127 us -> 123 us (0.969)
  starting transfers between devices: 56.3 us -> 48.5 us
  waiting for transfers between devices: 34.2 us -> 36.7 us
  other arithmetic: 0.98 us -> 2.57 us
    ppermute x7, starting transfers between devices: 29 us -> 21.4 us  [per_device(): block = lax.ppermute(block, ('x', 'c'), moves)]
    ppermute x7, waiting for transfers between devices: 6.32 us -> 13.2 us  [per_device(): block = lax.ppermute(block, ('x', 'c'), moves)]
    all_to_all x1, waiting for transfers between devices: 13.4 us -> 11.3 us  [per_device(): data = lax.all_to_all(data, 'tm', split_axis=0, concat_axis=0, tiled=True)]
    all_to_all x1, waiting for transfers between devices: 14.4 us -> 12.2 us  [per_device(): lax.all_to_all(rows, ('tm', 'x', 'c'), split_axis=0, concat_axis=0, tiled...]
    pallas_call x1, Pallas kernels: 3.31 us -> 1.66 us  [transform(): pl.pallas_call(kernel, in_specs=[whole()] * 2, out_specs=whole(), out_sha...]
    mul x1, other arithmetic: 0.21 us -> 1.79 us  [per_device(): masked = pseudo_inverse * active[:, :, None]]
    pallas_call x1, Pallas kernels: 0.68 us -> 2.18 us  [prepare(): pl.pallas_call(kernel, in_specs=[whole()] * peers + [pl.BlockSpec(memory_...]
  transfers between devices with their start and end apart: 9 -> 9, of which waited for: 4 -> 6; matrix products, arithmetic and copies ran while one was open for 0% -> 2% of each run, Pallas kernels for 1% -> 2%
where the time goes in v2:
time: 123 us
  starting transfers between devices  48.5 us (39%)
  waiting for transfers between devices  36.7 us (30%)
  blocking collectives  23.6 us (19%)
  Pallas kernels  8.05 us (7%)
  local copies, waits for them, and re-layouts  3.04 us (2%)
  other arithmetic  2.57 us (2%)
    all_to_all x1, blocking collectives, per_device(): lax.all_to_all(sky, ('x', 'h', 'c'), split_axis=0, concat_axis=0, tiled=T...  23.6 us
    ppermute x7, starting transfers between devices, per_device(): block = lax.ppermute(block, ('x', 'c'), moves)  21.4 us
    all_to_all x1, starting transfers between devices, per_device(): data = lax.all_to_all(data, 'tm', split_axis=0, concat_axis=0, tiled=True)  14 us
    ppermute x7, waiting for transfers between devices, per_device(): block = lax.ppermute(block, ('x', 'c'), moves)  13.2 us
    all_to_all x1, starting transfers between devices, per_device(): lax.all_to_all(rows, ('tm', 'x', 'c'), split_axis=0, concat_axis=0, tiled...  13.1 us
    all_to_all x1, waiting for transfers between devices, per_device(): lax.all_to_all(rows, ('tm', 'x', 'c'), split_axis=0, concat_axis=0, tiled...  12.2 us
    all_to_all x1, waiting for transfers between devices, per_device(): data = lax.all_to_all(data, 'tm', split_axis=0, concat_axis=0, tiled=True)  11.3 us
    pallas_call x1, Pallas kernels, by_baseline(): pl.pallas_call(kernel, in_specs=[pl.BlockSpec(memory_space=pl.ANY)], out_...  2.63 us
  transfers between devices with their start and end apart: 9, of which 6 were waited for; matrix products, arithmetic and copies ran while one was open for 2% of the time, Pallas kernels for 2%

profile of v2, /device:TPU:8, one launch (start us, length us, event | category | flops | bytes accessed | tf_op | source)
XLA Modules:
  0.0 122.9 jit_solution(7040471126487836116)
XLA Ops:
  0.0 2.6 %by_baseline.1 = bf16[32,128,256]{2,1,0:T(8,128)(2,1)} custom-call(bf16[128,64,128]{2,1,0:T(8,128)(2,1)} %in_ref.1), custom_call_target="tpu_custom_call" | custom-call | bytes 4194304 | tf_op jit(solution)/shard_map/by_baseline/pallas_call | solution.py:61
  2.6 0.0 copy-start.8
  2.7 0.0 copy-start.9
  2.7 14.0 %all-to-all-start = ((bf16[32,128,256]{2,1,0:T(8,128)(2,1)}), bf16[32,128,256]{2,1,0:T(8,128)(2,1)S(1)}, u32[]{:S(2)}, u32[]{:S(2)}) async-start(bf16[32,128,256]{2,1,0:T(8,128)(2,1)} %by_baseline.1), calls=%async_computation | async-start | bytes 4194304 | tf_op jit(solution)/shard_map/all_to_all | solution.py:223
  16.7 0.0 copy-done.8
  16.8 0.0 copy-done.9
  16.8 0.1 compare_convert_fusion
  16.8 1.8 %broadcast_multiply_fusion = bf16[16,64,1024]{2,1,0:T(8,128)(2,1)S(1)} fusion(bf16[16,64,1024]{2,1,0:T(8,128)(2,1)} %param.6, bf16[16,64]{1,0:T(8,128)(2,1)S(1)} %compare_convert_fusion), kind=kLoop, calls=%fused_computation | loop fusion | flops 1048576 | bytes 4196352 | tf_op jit(solution)/shard_map/mul | solution.py:227
  18.6 0.0 copy-start.1
  18.7 0.9 constant_dynamic-slice_fusion
  19.6 1.9 %collective-permute-start = (bf16[2,64,1024]{2,1,0:T(8,128)(2,1)S(1)}, bf16[2,64,1024]{2,1,0:T(8,128)(2,1)S(1)}, u32[]{:S(2)}, u32[]{:S(2)}) collective-permute-start(bf16[2,64,1024]{2,1,0:T(8,128)(2,1)S(1)} %get-tuple-element.29), channel_id=1, source_target_pairs={{0,1},{1,0},{4,5},{5,4},{8,9},{9,8},{12,13},{13,12},{2,3},{3,2},{6... | collective-permute-start | bytes 786440 | tf_op jit(solution)/shard_map/ppermute | solution.py:237
  21.5 3.4 %collective-permute-start.1 = (bf16[2,64,1024]{2,1,0:T(8,128)(2,1)S(1)}, bf16[2,64,1024]{2,1,0:T(8,128)(2,1)S(1)}, u32[]{:S(2)}, u32[]{:S(2)}) collective-permute-start(bf16[2,64,1024]{2,1,0:T(8,128)(2,1)S(1)} %get-tuple-element.28), channel_id=1, source_target_pairs={{0,4},{1,5},{4,8},{5,9},{8,12},{9,13},{12,0},{13,1},{2,6},{3,7},{6... | collective-permute-start | bytes 786440 | tf_op jit(solution)/shard_map/ppermute | solution.py:237
  24.9 3.2 %collective-permute-start.2 = (bf16[2,64,1024]{2,1,0:T(8,128)(2,1)S(1)}, bf16[2,64,1024]{2,1,0:T(8,128)(2,1)S(1)}, u32[]{:S(2)}, u32[]{:S(2)}) collective-permute-start(bf16[2,64,1024]{2,1,0:T(8,128)(2,1)S(1)} %get-tuple-element.27), channel_id=1, source_target_pairs={{0,5},{1,4},{4,9},{5,8},{8,13},{9,12},{12,1},{13,0},{2,7},{3,6},{6... | collective-permute-start | bytes 786440 | tf_op jit(solution)/shard_map/ppermute | solution.py:237
  28.1 3.6 %collective-permute-start.3 = (bf16[2,64,1024]{2,1,0:T(8,128)(2,1)S(1)}, bf16[2,64,1024]{2,1,0:T(8,128)(2,1)S(1)}, u32[]{:S(2)}, u32[]{:S(2)}) collective-permute-start(bf16[2,64,1024]{2,1,0:T(8,128)(2,1)S(1)} %get-tuple-element.26), channel_id=1, source_target_pairs={{0,8},{1,9},{4,12},{5,13},{8,0},{9,1},{12,4},{13,5},{2,10},{3,11},... | collective-permute-start | bytes 786440 | tf_op jit(solution)/shard_map/ppermute | solution.py:237
  31.7 3.3 %collective-permute-start.4 = (bf16[2,64,1024]{2,1,0:T(8,128)(2,1)S(1)}, bf16[2,64,1024]{2,1,0:T(8,128)(2,1)S(1)}, u32[]{:S(2)}, u32[]{:S(2)}) collective-permute-start(bf16[2,64,1024]{2,1,0:T(8,128)(2,1)S(1)} %get-tuple-element.25), channel_id=1, source_target_pairs={{0,9},{1,8},{4,13},{5,12},{8,1},{9,0},{12,5},{13,4},{2,11},{3,10},... | collective-permute-start | bytes 786440 | tf_op jit(solution)/shard_map/ppermute | solution.py:237
  35.1 0.0 collective-permute-done.refs_1_
  35.1 0.0 copy-start.2
  35.1 3.7 %collective-permute-start.5 = (bf16[2,64,1024]{2,1,0:T(8,128)(2,1)S(1)}, bf16[2,64,1024]{2,1,0:T(8,128)(2,1)S(1)}, u32[]{:S(2)}, u32[]{:S(2)}) collective-permute-start(bf16[2,64,1024]{2,1,0:T(8,128)(2,1)S(1)} %get-tuple-element.24), channel_id=1, source_target_pairs={{0,12},{1,13},{4,0},{5,1},{8,4},{9,5},{12,8},{13,9},{2,14},{3,15},... | collective-permute-start | bytes 786440 | tf_op jit(solution)/shard_map/ppermute | solution.py:237
  38.8 0.0 collective-permute-done.1.refs_2_
  38.8 0.0 copy-start.3
  38.8 2.3 %collective-permute-start.6 = (bf16[2,64,1024]{2,1,0:T(8,128)(2,1)S(1)}, bf16[2,64,1024]{2,1,0:T(8,128)(2,1)}, u32[]{:S(2)}, u32[]{:S(2)}) collective-permute-start(bf16[2,64,1024]{2,1,0:T(8,128)(2,1)S(1)} %get-tuple-element.23), channel_id=1, source_target_pairs={{0,13},{1,12},{4,1},{5,0},{8,5},{9,4},{12,9},{13,8},{2,15},{3,14},... | collective-permute-start | bytes 786440 | tf_op jit(solution)/shard_map/ppermute | solution.py:237
  41.1 0.0 collective-permute-done.2.refs_3_
  41.1 0.0 copy-start.4
  41.1 4.8 %collective-permute-done.3.refs_4_ = bf16[2,64,1024]{2,1,0:T(8,128)(2,1)S(1)} collective-permute-done((bf16[2,64,1024]{2,1,0:T(8,128)(2,1)S(1)}, bf16[2,64,1024]{2,1,0:T(8,128)(2,1)S(1)}, u32[]{:S(2)}, u32[]{:S(2)}) %collective-permute-start.3) | collective-permute-done | bytes 262176 | tf_op jit(solution)/shard_map/ppermute | solution.py:237
  45.9 0.0 copy-start.5
  45.9 4.8 %collective-permute-done.4.refs_5_ = bf16[2,64,1024]{2,1,0:T(8,128)(2,1)S(1)} collective-permute-done((bf16[2,64,1024]{2,1,0:T(8,128)(2,1)S(1)}, bf16[2,64,1024]{2,1,0:T(8,128)(2,1)S(1)}, u32[]{:S(2)}, u32[]{:S(2)}) %collective-permute-start.4) | collective-permute-done | bytes 262176 | tf_op jit(solution)/shard_map/ppermute | solution.py:237
  50.7 0.3 collective-permute-done.5.refs_6_
  51.0 0.0 copy-done.3
  51.0 0.0 copy-done.4
  51.0 0.0 copy-done.5
  51.0 0.4 copy-done.6
  51.4 0.7 copy-done.7
  52.1 3.3 %collective-permute-done.6.refs_7_ = bf16[2,64,1024]{2,1,0:T(8,128)(2,1)} collective-permute-done((bf16[2,64,1024]{2,1,0:T(8,128)(2,1)S(1)}, bf16[2,64,1024]{2,1,0:T(8,128)(2,1)}, u32[]{:S(2)}, u32[]{:S(2)}) %collective-permute-start.6) | collective-permute-done | bytes 262176 | tf_op jit(solution)/shard_map/ppermute | solution.py:237
  55.5 11.3 %all-to-all-done = bf16[32,128,256]{2,1,0:T(8,128)(2,1)S(1)} async-done(((bf16[32,128,256]{2,1,0:T(8,128)(2,1)}), bf16[32,128,256]{2,1,0:T(8,128)(2,1)S(1)}, u32[]{:S(2)}, u32[]{:S(2)}) %all-to-all-start) | async-done | bytes 2097184 | tf_op jit(solution)/shard_map/all_to_all | solution.py:223
  66.7 0.0 copy-done.2
  66.7 0.0 copy-done.1
  66.7 1.7 %transform.1.refs_8_ = bf16[512,256]{1,0:T(8,128)(2,1)S(1)} custom-call(bf16[528,1024]{1,0:T(8,128)(2,1)S(1)} %copy-done.1, bf16[4096,256]{1,0:T(8,128)(2,1)S(1)} %bitcast.11), custom_call_target="tpu_custom_call" | custom-call | flops 1107296256 | bytes 3178496 | tf_op jit(solution)/shard_map/transform/pallas_call | solution.py:149
  68.4 0.0 copy-start
  68.4 0.8 all_to_all.14
  69.2 13.1 %all-to-all-start.1 = ((bf16[256,2,256]{2,1,0:T(2,128)(2,1)}), bf16[256,2,256]{2,1,0:T(2,128)(2,1)S(1)}, u32[]{:S(2)}, u32[]{:S(2)}) async-start(bf16[256,2,256]{2,1,0:T(2,128)(2,1)} %all_to_all.14), calls=%async_computation.1 | async-start | bytes 524288 | tf_op jit(solution)/shard_map/all_to_all | solution.py:244
  82.4 0.1 stack.35.sources_ref
  82.5 0.0 copy-done
  82.5 2.2 %prepare.1.inverse_ref = bf16[2,512,1024]{2,1,0:T(8,128)(2,1)S(1)} custom-call(bf16[2,64,1024]{2,1,0:T(8,128)(2,1)} %get-tuple-element.15.refs_0_, bf16[2,64,1024]{2,1,0:T(8,128)(2,1)} %copy-done.2, bf16[2,64,1024]{2,1,0:T(8,128)(2,1)} %copy-done.3, bf16[2,64,1024]{2,1,0:T(8,128)(2,1)} %copy-done.4, bf16[2,64,1024]{2,1,0:T(8,128)(2,1)} %copy-done.5, ...), custom_call_target="tpu_custom_call" | custom-call | bytes 4194304 | tf_op jit(solution)/shard_map/prepare/pallas_call | solution.py:95
  84.7 12.2 %all-to-all-done.1 = bf16[256,2,256]{2,1,0:T(2,128)(2,1)S(1)} async-done(((bf16[256,2,256]{2,1,0:T(2,128)(2,1)}), bf16[256,2,256]{2,1,0:T(2,128)(2,1)S(1)}, u32[]{:S(2)}, u32[]{:S(2)}) %all-to-all-start.1) | async-done | bytes 262176 | tf_op jit(solution)/shard_map/all_to_all | solution.py:244
  96.9 0.1 all_to_all.16.rows_ref
  97.0 1.6 %product.1 = bf16[16,2,32,128]{3,2,1,0:T(8,128)(2,1)S(1)} custom-call(s32[8]{0:T(128)S(1)} %stack.35.sources_ref, bf16[512,256]{1,0:T(8,128)(2,1)S(1)} %all_to_all.16.rows_ref, bf16[2,512,1024]{2,1,0:T(8,128)(2,1)S(1)} %prepare.1.inverse_ref), custom_call_target="tpu_custom_call" | custom-call | flops 268435456 | bytes 2097152 | tf_op jit(solution)/shard_map/product/pallas_call | solution.py:191
  98.6 23.6 %all_to_all.21 = bf16[16,2,32,128]{3,2,1,0:T(8,128)(2,1)S(1)} all-to-all(bf16[16,2,32,128]{3,2,1,0:T(8,128)(2,1)S(1)} %product.1), channel_id=1, replica_groups=mesh['tm'=32,'x'=4,'h'=2,'c'=2] {'x','h','c'}, dimensions={0} | all-to-all | bytes 524288 | tf_op jit(solution)/shard_map/all_to_all | solution.py:247
  122.2 0.7 reduce
  (2 shorter events, 0.0 us)
Async XLA Ops:
  2.6 14.1 %copy-start.8 = (s32[64]{0:T(128)S(1)}, s32[64]{0:T(128)}, u32[]{:S(2)}) copy-start(s32[64]{0:T(128)} %param.7) | copy-start | bytes 772
  2.7 14.1 %copy-start.9 = (s32[16]{0:T(128)S(1)}, s32[16]{0:T(128)}, u32[]{:S(2)}) copy-start(s32[16]{0:T(128)} %param.8) | copy-start | bytes 196
  2.7 64.0 %all-to-all-start = ((bf16[32,128,256]{2,1,0:T(8,128)(2,1)}), bf16[32,128,256]{2,1,0:T(8,128)(2,1)S(1)}, u32[]{:S(2)}, u32[]{:S(2)}) async-start(bf16[32,128,256]{2,1,0:T(8,128)(2,1)} %by_baseline.1), calls=%async_computation | async-start | bytes 4194304 | tf_op jit(solution)/shard_map/all_to_all | solution.py:223
  18.6 48.1 %copy-start.1 = (bf16[528,1024]{1,0:T(8,128)(2,1)S(1)}, bf16[528,1024]{1,0:T(8,128)(2,1)}, u32[]{:S(2)}) copy-start(bf16[528,1024]{1,0:T(8,128)(2,1)} %constant.124.clone.table_ref) | copy-start | bytes 3244036
  19.6 15.5 %collective-permute-start = (bf16[2,64,1024]{2,1,0:T(8,128)(2,1)S(1)}, bf16[2,64,1024]{2,1,0:T(8,128)(2,1)S(1)}, u32[]{:S(2)}, u32[]{:S(2)}) collective-permute-start(bf16[2,64,1024]{2,1,0:T(8,128)(2,1)S(1)} %get-tuple-element.29), channel_id=1, source_target_pairs={{0,1},{1,0},{4,5},{5,4},{8,9},{9,8},{12,13},{13,12},{2,3},{3,2},{6... | collective-permute-start | bytes 786440 | tf_op jit(solution)/shard_map/ppermute | solution.py:237
  21.5 17.3 %collective-permute-start.1 = (bf16[2,64,1024]{2,1,0:T(8,128)(2,1)S(1)}, bf16[2,64,1024]{2,1,0:T(8,128)(2,1)S(1)}, u32[]{:S(2)}, u32[]{:S(2)}) collective-permute-start(bf16[2,64,1024]{2,1,0:T(8,128)(2,1)S(1)} %get-tuple-element.28), channel_id=1, source_target_pairs={{0,4},{1,5},{4,8},{5,9},{8,12},{9,13},{12,0},{13,1},{2,6},{3,7},{6... | collective-permute-start | bytes 786440 | tf_op jit(solution)/shard_map/ppermute | solution.py:237
  24.9 16.2 %collective-permute-start.2 = (bf16[2,64,1024]{2,1,0:T(8,128)(2,1)S(1)}, bf16[2,64,1024]{2,1,0:T(8,128)(2,1)S(1)}, u32[]{:S(2)}, u32[]{:S(2)}) collective-permute-start(bf16[2,64,1024]{2,1,0:T(8,128)(2,1)S(1)} %get-tuple-element.27), channel_id=1, source_target_pairs={{0,5},{1,4},{4,9},{5,8},{8,13},{9,12},{12,1},{13,0},{2,7},{3,6},{6... | collective-permute-start | bytes 786440 | tf_op jit(solution)/shard_map/ppermute | solution.py:237
  28.1 17.8 %collective-permute-start.3 = (bf16[2,64,1024]{2,1,0:T(8,128)(2,1)S(1)}, bf16[2,64,1024]{2,1,0:T(8,128)(2,1)S(1)}, u32[]{:S(2)}, u32[]{:S(2)}) collective-permute-start(bf16[2,64,1024]{2,1,0:T(8,128)(2,1)S(1)} %get-tuple-element.26), channel_id=1, source_target_pairs={{0,8},{1,9},{4,12},{5,13},{8,0},{9,1},{12,4},{13,5},{2,10},{3,11},... | collective-permute-start | bytes 786440 | tf_op jit(solution)/shard_map/ppermute | solution.py:237
  31.7 19.0 %collective-permute-start.4 = (bf16[2,64,1024]{2,1,0:T(8,128)(2,1)S(1)}, bf16[2,64,1024]{2,1,0:T(8,128)(2,1)S(1)}, u32[]{:S(2)}, u32[]{:S(2)}) collective-permute-start(bf16[2,64,1024]{2,1,0:T(8,128)(2,1)S(1)} %get-tuple-element.25), channel_id=1, source_target_pairs={{0,9},{1,8},{4,13},{5,12},{8,1},{9,0},{12,5},{13,4},{2,11},{3,10},... | collective-permute-start | bytes 786440 | tf_op jit(solution)/shard_map/ppermute | solution.py:237
  35.1 31.6 %copy-start.2 = (bf16[2,64,1024]{2,1,0:T(8,128)(2,1)}, bf16[2,64,1024]{2,1,0:T(8,128)(2,1)S(1)}, u32[]{:S(2)}) copy-start(bf16[2,64,1024]{2,1,0:T(8,128)(2,1)S(1)} %collective-permute-done.refs_1_) | copy-start | bytes 786436
  35.1 15.9 %collective-permute-start.5 = (bf16[2,64,1024]{2,1,0:T(8,128)(2,1)S(1)}, bf16[2,64,1024]{2,1,0:T(8,128)(2,1)S(1)}, u32[]{:S(2)}, u32[]{:S(2)}) collective-permute-start(bf16[2,64,1024]{2,1,0:T(8,128)(2,1)S(1)} %get-tuple-element.24), channel_id=1, source_target_pairs={{0,12},{1,13},{4,0},{5,1},{8,4},{9,5},{12,8},{13,9},{2,14},{3,15},... | collective-permute-start | bytes 786440 | tf_op jit(solution)/shard_map/ppermute | solution.py:237
  38.8 12.2 %copy-start.3 = (bf16[2,64,1024]{2,1,0:T(8,128)(2,1)}, bf16[2,64,1024]{2,1,0:T(8,128)(2,1)S(1)}, u32[]{:S(2)}) copy-start(bf16[2,64,1024]{2,1,0:T(8,128)(2,1)S(1)} %collective-permute-done.1.refs_2_) | copy-start | bytes 786436
  38.8 16.7 %collective-permute-start.6 = (bf16[2,64,1024]{2,1,0:T(8,128)(2,1)S(1)}, bf16[2,64,1024]{2,1,0:T(8,128)(2,1)}, u32[]{:S(2)}, u32[]{:S(2)}) collective-permute-start(bf16[2,64,1024]{2,1,0:T(8,128)(2,1)S(1)} %get-tuple-element.23), channel_id=1, source_target_pairs={{0,13},{1,12},{4,1},{5,0},{8,5},{9,4},{12,9},{13,8},{2,15},{3,14},... | collective-permute-start | bytes 786440 | tf_op jit(solution)/shard_map/ppermute | solution.py:237
  41.1 9.9 %copy-start.4 = (bf16[2,64,1024]{2,1,0:T(8,128)(2,1)}, bf16[2,64,1024]{2,1,0:T(8,128)(2,1)S(1)}, u32[]{:S(2)}) copy-start(bf16[2,64,1024]{2,1,0:T(8,128)(2,1)S(1)} %collective-permute-done.2.refs_3_) | copy-start | bytes 786436
  45.9 5.1 %copy-start.5 = (bf16[2,64,1024]{2,1,0:T(8,128)(2,1)}, bf16[2,64,1024]{2,1,0:T(8,128)(2,1)S(1)}, u32[]{:S(2)}) copy-start(bf16[2,64,1024]{2,1,0:T(8,128)(2,1)S(1)} %collective-permute-done.3.refs_4_) | copy-start | bytes 786436
  50.7 0.7 copy-start.6
  51.4 0.7 copy-start.7
  68.4 14.1 %copy-start = (bf16[512,256]{1,0:T(8,128)(2,1)}, bf16[512,256]{1,0:T(8,128)(2,1)S(1)}, u32[]{:S(2)}) copy-start(bf16[512,256]{1,0:T(8,128)(2,1)S(1)} %transform.1.refs_8_) | copy-start | bytes 786436
  69.2 27.7 %all-to-all-start.1 = ((bf16[256,2,256]{2,1,0:T(2,128)(2,1)}), bf16[256,2,256]{2,1,0:T(2,128)(2,1)S(1)}, u32[]{:S(2)}, u32[]{:S(2)}) async-start(bf16[256,2,256]{2,1,0:T(2,128)(2,1)} %all_to_all.14), calls=%async_computation.1 | async-start | bytes 524288 | tf_op jit(solution)/shard_map/all_to_all | solution.py:244

commit v3 on v2

--- a/solution.py
+++ b/solution.py
@@ -107,6 +107,7 @@
 
 def transform(data, modes, ns):
     samples, width = data.shape
+    per_b = width // (2 * ns)
     quarter, half = samples // 4, modes // 2
     scale = 1.0 / math.sqrt(samples)
     table = tables(modes, samples)
@@ -117,7 +118,7 @@
             parts += [v[:, b + ns : b + 2 * ns], -v[:, b : b + ns]]
         return jnp.concatenate(parts, axis=1)
 
-    def kernel(table_ref, data_ref, out_ref):
+    def kernel(table_ref, data_ref, out_ref, wide):
         z = [
             jnp.dot(
                 table_ref[...],
@@ -141,16 +142,19 @@
         minus = jnp.where(row == 0, last, minus).astype(jnp.bfloat16)
         both = sum(lax.broadcasted_iota(jnp.int32, (half, half), d) for d in (0, 1))
         back = jnp.where(both % half == 0, 1.0, 0.0).astype(jnp.bfloat16)
-        out_ref[:half, :] = jnp.dot(
-            back, minus, preferred_element_type=jnp.float32
-        ).astype(jnp.bfloat16)
-        out_ref[half:, :] = plus.astype(jnp.bfloat16)
+        minus = jnp.dot(back, minus, preferred_element_type=jnp.float32)
+        for i, value in enumerate((minus, plus)):
+            for b in range(per_b):
+                to = pl.ds(i * half * per_b + b, half, stride=per_b)
+                wide[to, :] = value[:, b * 2 * ns : (b + 1) * 2 * ns]
+        out_ref[...] = wide[...].astype(jnp.bfloat16)
 
     return pl.pallas_call(
         kernel,
         in_specs=[whole()] * 2,
         out_specs=whole(),
-        out_shape=jax.ShapeDtypeStruct((modes, width), jnp.bfloat16),
+        out_shape=jax.ShapeDtypeStruct((modes * per_b, 2 * ns), jnp.bfloat16),
+        scratch_shapes=[pltpu.VMEM((modes * per_b, 2 * ns), jnp.float32)],
         compiler_params=pltpu.CompilerParams(vmem_limit_bytes=12 * MIB),
         cost_estimate=pl.CostEstimate(
             flops=2 * table.size * 4 * width,
@@ -164,24 +168,19 @@
 def product(inverse, rows, sources, devices, ns):
     each_m, harm, _ = inverse.shape
     n_rows, width = rows.shape
-    peers = sources.shape[0]
-    outer = n_rows // (each_m * peers)
-    bits = [n.bit_length() - 1 for n in (outer, peers)]
+    peers, per_b = sources.shape[0], 2
+    step = peers * each_m * per_b
+    outer = n_rows // step
     per = harm // devices
 
-    def kernel(sources_ref, rows_ref, inverse_ref, out_ref, sorted_rows):
-        to = lax.broadcasted_iota(jnp.int32, (n_rows, 1), 0)
-        o, p, m = to & (outer - 1), (to >> bits[0]) & (peers - 1), to >> (bits[0] + bits[1])
-        source = (o * peers + p) * each_m + m
-        column = lax.broadcasted_iota(jnp.int32, (n_rows, n_rows), 1)
-        matrix = jnp.where(column == source, 1.0, 0.0).astype(jnp.bfloat16)
-        sorted_rows[...] = jnp.dot(matrix, rows_ref[...], preferred_element_type=jnp.float32)
+    def kernel(sources_ref, rows_ref, inverse_ref, out_ref, wide):
+        wide[...] = rows_ref[...].astype(jnp.float32)
         for m in range(each_m):
             plain, turned = [], []
             for p in range(peers):
-                at = pl.multiple_of((m * peers + sources_ref[p]) * outer, outer)
-                for h in range(0, width, 2 * ns):
-                    one = sorted_rows[pl.ds(at, outer), h : h + 2 * ns]
+                for b in range(per_b):
+                    start = (sources_ref[p] * each_m + m) * per_b + b
+                    one = wide[pl.ds(start, outer, stride=step), :]
                     plain.append(one)
                     turned.append(jnp.concatenate([-one[:, ns:], one[:, :ns]], axis=1))
             weights = jnp.concatenate(plain + turned, axis=0).astype(jnp.bfloat16)

time: 123 us -> 123 us (level)
  no operation moved by 1% of the time
where the time goes in v3:
time: 123 us
  starting transfers between devices  48.5 us (39%)
  waiting for transfers between devices  36.7 us (30%)
  blocking collectives  23.6 us (19%)
  Pallas kernels  8.72 us (7%)
  other arithmetic  2.57 us (2%)
  local copies, waits for them, and re-layouts  2.17 us (2%)
    all_to_all x1, blocking collectives, per_device(): lax.all_to_all(sky, ('x', 'h', 'c'), split_axis=0, concat_axis=0, tiled=T...  23.6 us
    ppermute x7, starting transfers between devices, per_device(): block = lax.ppermute(block, ('x', 'c'), moves)  21.4 us
    all_to_all x1, starting transfers between devices, per_device(): data = lax.all_to_all(data, 'tm', split_axis=0, concat_axis=0, tiled=True)  14 us
    ppermute x7, waiting for transfers between devices, per_device(): block = lax.ppermute(block, ('x', 'c'), moves)  13.2 us
    all_to_all x1, starting transfers between devices, per_device(): lax.all_to_all(rows, ('tm', 'x', 'c'), split_axis=0, concat_axis=0, tiled...  13.1 us
    all_to_all x1, waiting for transfers between devices, per_device(): lax.all_to_all(rows, ('tm', 'x', 'c'), split_axis=0, concat_axis=0, tiled...  12.2 us
    all_to_all x1, waiting for transfers between devices, per_device(): data = lax.all_to_all(data, 'tm', split_axis=0, concat_axis=0, tiled=True)  11.2 us
    pallas_call x1, Pallas kernels, by_baseline(): pl.pallas_call(kernel, in_specs=[pl.BlockSpec(memory_space=pl.ANY)], out_...  2.62 us
  transfers between devices with their start and end apart: 9, of which 6 were waited for; matrix products, arithmetic and copies ran while one was open for 2% of the time, Pallas kernels for 2%

profile of v3, /device:TPU:8, one launch (start us, length us, event | category | flops | bytes accessed | tf_op | source)
XLA Modules:
  0.0 122.6 jit_solution(10783637122002563234)
XLA Ops:
  0.0 2.6 %by_baseline.1 = bf16[32,128,256]{2,1,0:T(8,128)(2,1)} custom-call(bf16[128,64,128]{2,1,0:T(8,128)(2,1)} %in_ref.1), custom_call_target="tpu_custom_call" | custom-call | bytes 4194304 | tf_op jit(solution)/shard_map/by_baseline/pallas_call | solution.py:61
  2.6 0.0 copy-start.7
  2.6 0.0 copy-start.8
  2.7 14.0 %all-to-all-start = ((bf16[32,128,256]{2,1,0:T(8,128)(2,1)}), bf16[32,128,256]{2,1,0:T(8,128)(2,1)S(1)}, u32[]{:S(2)}, u32[]{:S(2)}) async-start(bf16[32,128,256]{2,1,0:T(8,128)(2,1)} %by_baseline.1), calls=%async_computation | async-start | bytes 4194304 | tf_op jit(solution)/shard_map/all_to_all | solution.py:222
  16.7 0.0 copy-done.7
  16.7 0.0 copy-done.8
  16.8 0.1 compare_convert_fusion
  16.8 1.8 %broadcast_multiply_fusion = bf16[16,64,1024]{2,1,0:T(8,128)(2,1)S(1)} fusion(bf16[16,64,1024]{2,1,0:T(8,128)(2,1)} %param.6, bf16[16,64]{1,0:T(8,128)(2,1)S(1)} %compare_convert_fusion), kind=kLoop, calls=%fused_computation | loop fusion | flops 1048576 | bytes 4196352 | tf_op jit(solution)/shard_map/mul | solution.py:226
  18.6 0.0 copy-start
  18.6 0.9 constant_dynamic-slice_fusion
  19.5 1.9 %collective-permute-start = (bf16[2,64,1024]{2,1,0:T(8,128)(2,1)S(1)}, bf16[2,64,1024]{2,1,0:T(8,128)(2,1)S(1)}, u32[]{:S(2)}, u32[]{:S(2)}) collective-permute-start(bf16[2,64,1024]{2,1,0:T(8,128)(2,1)S(1)} %get-tuple-element.29), channel_id=1, source_target_pairs={{0,1},{1,0},{4,5},{5,4},{8,9},{9,8},{12,13},{13,12},{2,3},{3,2},{6... | collective-permute-start | bytes 786440 | tf_op jit(solution)/shard_map/ppermute | solution.py:236
  21.5 3.4 %collective-permute-start.1 = (bf16[2,64,1024]{2,1,0:T(8,128)(2,1)S(1)}, bf16[2,64,1024]{2,1,0:T(8,128)(2,1)S(1)}, u32[]{:S(2)}, u32[]{:S(2)}) collective-permute-start(bf16[2,64,1024]{2,1,0:T(8,128)(2,1)S(1)} %get-tuple-element.28), channel_id=1, source_target_pairs={{0,4},{1,5},{4,8},{5,9},{8,12},{9,13},{12,0},{13,1},{2,6},{3,7},{6... | collective-permute-start | bytes 786440 | tf_op jit(solution)/shard_map/ppermute | solution.py:236
  24.9 3.2 %collective-permute-start.2 = (bf16[2,64,1024]{2,1,0:T(8,128)(2,1)S(1)}, bf16[2,64,1024]{2,1,0:T(8,128)(2,1)S(1)}, u32[]{:S(2)}, u32[]{:S(2)}) collective-permute-start(bf16[2,64,1024]{2,1,0:T(8,128)(2,1)S(1)} %get-tuple-element.27), channel_id=1, source_target_pairs={{0,5},{1,4},{4,9},{5,8},{8,13},{9,12},{12,1},{13,0},{2,7},{3,6},{6... | collective-permute-start | bytes 786440 | tf_op jit(solution)/shard_map/ppermute | solution.py:236
  28.1 3.6 %collective-permute-start.3 = (bf16[2,64,1024]{2,1,0:T(8,128)(2,1)S(1)}, bf16[2,64,1024]{2,1,0:T(8,128)(2,1)S(1)}, u32[]{:S(2)}, u32[]{:S(2)}) collective-permute-start(bf16[2,64,1024]{2,1,0:T(8,128)(2,1)S(1)} %get-tuple-element.26), channel_id=1, source_target_pairs={{0,8},{1,9},{4,12},{5,13},{8,0},{9,1},{12,4},{13,5},{2,10},{3,11},... | collective-permute-start | bytes 786440 | tf_op jit(solution)/shard_map/ppermute | solution.py:236
  31.7 3.3 %collective-permute-start.4 = (bf16[2,64,1024]{2,1,0:T(8,128)(2,1)S(1)}, bf16[2,64,1024]{2,1,0:T(8,128)(2,1)S(1)}, u32[]{:S(2)}, u32[]{:S(2)}) collective-permute-start(bf16[2,64,1024]{2,1,0:T(8,128)(2,1)S(1)} %get-tuple-element.25), channel_id=1, source_target_pairs={{0,9},{1,8},{4,13},{5,12},{8,1},{9,0},{12,5},{13,4},{2,11},{3,10},... | collective-permute-start | bytes 786440 | tf_op jit(solution)/shard_map/ppermute | solution.py:236
  35.1 0.0 collective-permute-done.refs_1_
  35.1 0.0 copy-start.1
  35.1 3.7 %collective-permute-start.5 = (bf16[2,64,1024]{2,1,0:T(8,128)(2,1)S(1)}, bf16[2,64,1024]{2,1,0:T(8,128)(2,1)S(1)}, u32[]{:S(2)}, u32[]{:S(2)}) collective-permute-start(bf16[2,64,1024]{2,1,0:T(8,128)(2,1)S(1)} %get-tuple-element.24), channel_id=1, source_target_pairs={{0,12},{1,13},{4,0},{5,1},{8,4},{9,5},{12,8},{13,9},{2,14},{3,15},... | collective-permute-start | bytes 786440 | tf_op jit(solution)/shard_map/ppermute | solution.py:236
  38.8 0.0 collective-permute-done.1.refs_2_
  38.8 0.0 copy-start.2
  38.8 2.3 %collective-permute-start.6 = (bf16[2,64,1024]{2,1,0:T(8,128)(2,1)S(1)}, bf16[2,64,1024]{2,1,0:T(8,128)(2,1)}, u32[]{:S(2)}, u32[]{:S(2)}) collective-permute-start(bf16[2,64,1024]{2,1,0:T(8,128)(2,1)S(1)} %get-tuple-element.23), channel_id=1, source_target_pairs={{0,13},{1,12},{4,1},{5,0},{8,5},{9,4},{12,9},{13,8},{2,15},{3,14},... | collective-permute-start | bytes 786440 | tf_op jit(solution)/shard_map/ppermute | solution.py:236
  41.1 0.0 collective-permute-done.2.refs_3_
  41.1 0.0 copy-start.3
  41.1 4.8 %collective-permute-done.3.refs_4_ = bf16[2,64,1024]{2,1,0:T(8,128)(2,1)S(1)} collective-permute-done((bf16[2,64,1024]{2,1,0:T(8,128)(2,1)S(1)}, bf16[2,64,1024]{2,1,0:T(8,128)(2,1)S(1)}, u32[]{:S(2)}, u32[]{:S(2)}) %collective-permute-start.3) | collective-permute-done | bytes 262176 | tf_op jit(solution)/shard_map/ppermute | solution.py:236
  45.9 0.0 copy-start.4
  45.9 4.8 %collective-permute-done.4.refs_5_ = bf16[2,64,1024]{2,1,0:T(8,128)(2,1)S(1)} collective-permute-done((bf16[2,64,1024]{2,1,0:T(8,128)(2,1)S(1)}, bf16[2,64,1024]{2,1,0:T(8,128)(2,1)S(1)}, u32[]{:S(2)}, u32[]{:S(2)}) %collective-permute-start.4) | collective-permute-done | bytes 262176 | tf_op jit(solution)/shard_map/ppermute | solution.py:236
  50.7 0.0 copy-start.5
  50.7 0.3 collective-permute-done.5.refs_6_
  51.0 0.0 copy-done.2
  51.0 0.0 copy-done.3
  51.0 0.0 copy-done.4
  51.0 0.4 copy-done.5
  51.4 0.0 copy-start.6
  51.4 0.7 copy-done.6
  52.1 3.3 %collective-permute-done.6.refs_7_ = bf16[2,64,1024]{2,1,0:T(8,128)(2,1)} collective-permute-done((bf16[2,64,1024]{2,1,0:T(8,128)(2,1)S(1)}, bf16[2,64,1024]{2,1,0:T(8,128)(2,1)}, u32[]{:S(2)}, u32[]{:S(2)}) %collective-permute-start.6) | collective-permute-done | bytes 262176 | tf_op jit(solution)/shard_map/ppermute | solution.py:236
  55.4 11.2 %all-to-all-done = bf16[32,128,256]{2,1,0:T(8,128)(2,1)S(1)} async-done(((bf16[32,128,256]{2,1,0:T(8,128)(2,1)}), bf16[32,128,256]{2,1,0:T(8,128)(2,1)S(1)}, u32[]{:S(2)}, u32[]{:S(2)}) %all-to-all-start) | async-done | bytes 2097184 | tf_op jit(solution)/shard_map/all_to_all | solution.py:222
  66.7 0.0 copy-done
  66.7 2.4 %transform.1.refs_8_ = bf16[1024,128]{1,0:T(8,128)(2,1)} custom-call(bf16[528,1024]{1,0:T(8,128)(2,1)S(1)} %copy-done, bf16[4096,256]{1,0:T(8,128)(2,1)S(1)} %bitcast.13), custom_call_target="tpu_custom_call" | custom-call | flops 1107296256 | bytes 3178496 | tf_op jit(solution)/shard_map/transform/pallas_call | solution.py:152
  69.1 0.0 copy-done.1
  69.1 13.1 %all-to-all-start.1 = ((bf16[256,4,128]{2,1,0:T(4,128)(2,1)}), bf16[256,4,128]{2,1,0:T(4,128)(2,1)S(1)}, u32[]{:S(2)}, u32[]{:S(2)}) async-start(bf16[256,4,128]{2,1,0:T(4,128)(2,1)} %bitcast.9), calls=%async_computation.1 | async-start | bytes 524288 | tf_op jit(solution)/shard_map/all_to_all | solution.py:243
  82.3 0.1 stack.35.sources_ref
  82.4 2.2 %prepare.1.inverse_ref = bf16[2,512,1024]{2,1,0:T(8,128)(2,1)S(1)} custom-call(bf16[2,64,1024]{2,1,0:T(8,128)(2,1)} %get-tuple-element.15.refs_0_, bf16[2,64,1024]{2,1,0:T(8,128)(2,1)} %copy-done.1, bf16[2,64,1024]{2,1,0:T(8,128)(2,1)} %copy-done.2, bf16[2,64,1024]{2,1,0:T(8,128)(2,1)} %copy-done.3, bf16[2,64,1024]{2,1,0:T(8,128)(2,1)} %copy-done.4, ...), custom_call_target="tpu_custom_call" | custom-call | bytes 4194304 | tf_op jit(solution)/shard_map/prepare/pallas_call | solution.py:95
  84.6 12.2 %all-to-all-done.1 = bf16[256,4,128]{2,1,0:T(4,128)(2,1)S(1)} async-done(((bf16[256,4,128]{2,1,0:T(4,128)(2,1)}), bf16[256,4,128]{2,1,0:T(4,128)(2,1)S(1)}, u32[]{:S(2)}, u32[]{:S(2)}) %all-to-all-start.1) | async-done | bytes 262176 | tf_op jit(solution)/shard_map/all_to_all | solution.py:243
  96.8 1.5 %product.1 = bf16[16,2,32,128]{3,2,1,0:T(8,128)(2,1)S(1)} custom-call(s32[8]{0:T(128)S(1)} %stack.35.sources_ref, bf16[1024,128]{1,0:T(8,128)(2,1)S(1)} %bitcast.14, bf16[2,512,1024]{2,1,0:T(8,128)(2,1)S(1)} %prepare.1.inverse_ref), custom_call_target="tpu_custom_call" | custom-call | flops 268435456 | bytes 2097152 | tf_op jit(solution)/shard_map/product/pallas_call | solution.py:190
  98.3 23.6 %all_to_all.21 = bf16[16,2,32,128]{3,2,1,0:T(8,128)(2,1)S(1)} all-to-all(bf16[16,2,32,128]{3,2,1,0:T(8,128)(2,1)S(1)} %product.1), channel_id=1, replica_groups=mesh['tm'=32,'x'=4,'h'=2,'c'=2] {'x','h','c'}, dimensions={0} | all-to-all | bytes 524288 | tf_op jit(solution)/shard_map/all_to_all | solution.py:246
  121.9 0.7 reduce
Async XLA Ops:
  2.6 14.1 %copy-start.7 = (s32[64]{0:T(128)S(1)}, s32[64]{0:T(128)}, u32[]{:S(2)}) copy-start(s32[64]{0:T(128)} %param.7) | copy-start | bytes 772
  2.6 14.1 %copy-start.8 = (s32[16]{0:T(128)S(1)}, s32[16]{0:T(128)}, u32[]{:S(2)}) copy-start(s32[16]{0:T(128)} %param.8) | copy-start | bytes 196
  2.7 64.0 %all-to-all-start = ((bf16[32,128,256]{2,1,0:T(8,128)(2,1)}), bf16[32,128,256]{2,1,0:T(8,128)(2,1)S(1)}, u32[]{:S(2)}, u32[]{:S(2)}) async-start(bf16[32,128,256]{2,1,0:T(8,128)(2,1)} %by_baseline.1), calls=%async_computation | async-start | bytes 4194304 | tf_op jit(solution)/shard_map/all_to_all | solution.py:222
  18.6 48.1 %copy-start = (bf16[528,1024]{1,0:T(8,128)(2,1)S(1)}, bf16[528,1024]{1,0:T(8,128)(2,1)}, u32[]{:S(2)}) copy-start(bf16[528,1024]{1,0:T(8,128)(2,1)} %constant.124.clone.table_ref) | copy-start | bytes 3244036
  19.5 15.5 %collective-permute-start = (bf16[2,64,1024]{2,1,0:T(8,128)(2,1)S(1)}, bf16[2,64,1024]{2,1,0:T(8,128)(2,1)S(1)}, u32[]{:S(2)}, u32[]{:S(2)}) collective-permute-start(bf16[2,64,1024]{2,1,0:T(8,128)(2,1)S(1)} %get-tuple-element.29), channel_id=1, source_target_pairs={{0,1},{1,0},{4,5},{5,4},{8,9},{9,8},{12,13},{13,12},{2,3},{3,2},{6... | collective-permute-start | bytes 786440 | tf_op jit(solution)/shard_map/ppermute | solution.py:236
  21.5 17.3 %collective-permute-start.1 = (bf16[2,64,1024]{2,1,0:T(8,128)(2,1)S(1)}, bf16[2,64,1024]{2,1,0:T(8,128)(2,1)S(1)}, u32[]{:S(2)}, u32[]{:S(2)}) collective-permute-start(bf16[2,64,1024]{2,1,0:T(8,128)(2,1)S(1)} %get-tuple-element.28), channel_id=1, source_target_pairs={{0,4},{1,5},{4,8},{5,9},{8,12},{9,13},{12,0},{13,1},{2,6},{3,7},{6... | collective-permute-start | bytes 786440 | tf_op jit(solution)/shard_map/ppermute | solution.py:236
  24.9 16.2 %collective-permute-start.2 = (bf16[2,64,1024]{2,1,0:T(8,128)(2,1)S(1)}, bf16[2,64,1024]{2,1,0:T(8,128)(2,1)S(1)}, u32[]{:S(2)}, u32[]{:S(2)}) collective-permute-start(bf16[2,64,1024]{2,1,0:T(8,128)(2,1)S(1)} %get-tuple-element.27), channel_id=1, source_target_pairs={{0,5},{1,4},{4,9},{5,8},{8,13},{9,12},{12,1},{13,0},{2,7},{3,6},{6... | collective-permute-start | bytes 786440 | tf_op jit(solution)/shard_map/ppermute | solution.py:236
  28.1 17.8 %collective-permute-start.3 = (bf16[2,64,1024]{2,1,0:T(8,128)(2,1)S(1)}, bf16[2,64,1024]{2,1,0:T(8,128)(2,1)S(1)}, u32[]{:S(2)}, u32[]{:S(2)}) collective-permute-start(bf16[2,64,1024]{2,1,0:T(8,128)(2,1)S(1)} %get-tuple-element.26), channel_id=1, source_target_pairs={{0,8},{1,9},{4,12},{5,13},{8,0},{9,1},{12,4},{13,5},{2,10},{3,11},... | collective-permute-start | bytes 786440 | tf_op jit(solution)/shard_map/ppermute | solution.py:236
  31.7 19.0 %collective-permute-start.4 = (bf16[2,64,1024]{2,1,0:T(8,128)(2,1)S(1)}, bf16[2,64,1024]{2,1,0:T(8,128)(2,1)S(1)}, u32[]{:S(2)}, u32[]{:S(2)}) collective-permute-start(bf16[2,64,1024]{2,1,0:T(8,128)(2,1)S(1)} %get-tuple-element.25), channel_id=1, source_target_pairs={{0,9},{1,8},{4,13},{5,12},{8,1},{9,0},{12,5},{13,4},{2,11},{3,10},... | collective-permute-start | bytes 786440 | tf_op jit(solution)/shard_map/ppermute | solution.py:236
  35.1 34.0 %copy-start.1 = (bf16[2,64,1024]{2,1,0:T(8,128)(2,1)}, bf16[2,64,1024]{2,1,0:T(8,128)(2,1)S(1)}, u32[]{:S(2)}) copy-start(bf16[2,64,1024]{2,1,0:T(8,128)(2,1)S(1)} %collective-permute-done.refs_1_) | copy-start | bytes 786436
  35.1 15.9 %collective-permute-start.5 = (bf16[2,64,1024]{2,1,0:T(8,128)(2,1)S(1)}, bf16[2,64,1024]{2,1,0:T(8,128)(2,1)S(1)}, u32[]{:S(2)}, u32[]{:S(2)}) collective-permute-start(bf16[2,64,1024]{2,1,0:T(8,128)(2,1)S(1)} %get-tuple-element.24), channel_id=1, source_target_pairs={{0,12},{1,13},{4,0},{5,1},{8,4},{9,5},{12,8},{13,9},{2,14},{3,15},... | collective-permute-start | bytes 786440 | tf_op jit(solution)/shard_map/ppermute | solution.py:236
  38.8 12.2 %copy-start.2 = (bf16[2,64,1024]{2,1,0:T(8,128)(2,1)}, bf16[2,64,1024]{2,1,0:T(8,128)(2,1)S(1)}, u32[]{:S(2)}) copy-start(bf16[2,64,1024]{2,1,0:T(8,128)(2,1)S(1)} %collective-permute-done.1.refs_2_) | copy-start | bytes 786436
  38.8 16.7 %collective-permute-start.6 = (bf16[2,64,1024]{2,1,0:T(8,128)(2,1)S(1)}, bf16[2,64,1024]{2,1,0:T(8,128)(2,1)}, u32[]{:S(2)}, u32[]{:S(2)}) collective-permute-start(bf16[2,64,1024]{2,1,0:T(8,128)(2,1)S(1)} %get-tuple-element.23), channel_id=1, source_target_pairs={{0,13},{1,12},{4,1},{5,0},{8,5},{9,4},{12,9},{13,8},{2,15},{3,14},... | collective-permute-start | bytes 786440 | tf_op jit(solution)/shard_map/ppermute | solution.py:236
  41.1 9.9 %copy-start.3 = (bf16[2,64,1024]{2,1,0:T(8,128)(2,1)}, bf16[2,64,1024]{2,1,0:T(8,128)(2,1)S(1)}, u32[]{:S(2)}) copy-start(bf16[2,64,1024]{2,1,0:T(8,128)(2,1)S(1)} %collective-permute-done.2.refs_3_) | copy-start | bytes 786436
  45.9 5.1 %copy-start.4 = (bf16[2,64,1024]{2,1,0:T(8,128)(2,1)}, bf16[2,64,1024]{2,1,0:T(8,128)(2,1)S(1)}, u32[]{:S(2)}) copy-start(bf16[2,64,1024]{2,1,0:T(8,128)(2,1)S(1)} %collective-permute-done.3.refs_4_) | copy-start | bytes 786436
  50.7 0.7 copy-start.5
  51.4 0.7 copy-start.6
  69.1 27.7 %all-to-all-start.1 = ((bf16[256,4,128]{2,1,0:T(4,128)(2,1)}), bf16[256,4,128]{2,1,0:T(4,128)(2,1)S(1)}, u32[]{:S(2)}, u32[]{:S(2)}) async-start(bf16[256,4,128]{2,1,0:T(4,128)(2,1)} %bitcast.9), calls=%async_computation.1 | async-start | bytes 524288 | tf_op jit(solution)/shard_map/all_to_all | solution.py:243

commit v4 on v3

--- a/solution.py
+++ b/solution.py
@@ -30,7 +30,7 @@
 
 def by_baseline(visibilities):
     times, baselines, width = visibilities.shape
-    half, tile, block = baselines // 2, 16, 32
+    half, tile, block = baselines // 2, 16, 16
     blocks = times // block
 
     def kernel(in_ref, out_ref, near, turned, in_sems, out_sems):

time: 123 us -> 123 us (level)
  no operation moved by 1% of the time
where the time goes in v4:
time: 123 us
  starting transfers between devices  48.5 us (39%)
  waiting for transfers between devices  36.7 us (30%)
  blocking collectives  23.6 us (19%)
  Pallas kernels  8.65 us (7%)
  other arithmetic  2.57 us (2%)
  local copies, waits for them, and re-layouts  2.17 us (2%)
    all_to_all x1, blocking collectives, per_device(): lax.all_to_all(sky, ('x', 'h', 'c'), split_axis=0, concat_axis=0, tiled=T...  23.6 us
    ppermute x7, starting transfers between devices, per_device(): block = lax.ppermute(block, ('x', 'c'), moves)  21.4 us
    all_to_all x1, starting transfers between devices, per_device(): data = lax.all_to_all(data, 'tm', split_axis=0, concat_axis=0, tiled=True)  14 us
    ppermute x7, waiting for transfers between devices, per_device(): block = lax.ppermute(block, ('x', 'c'), moves)  13.2 us
    all_to_all x1, starting transfers between devices, per_device(): lax.all_to_all(rows, ('tm', 'x', 'c'), split_axis=0, concat_axis=0, tiled...  13.1 us
    all_to_all x1, waiting for transfers between devices, per_device(): lax.all_to_all(rows, ('tm', 'x', 'c'), split_axis=0, concat_axis=0, tiled...  12.2 us
    all_to_all x1, waiting for transfers between devices, per_device(): data = lax.all_to_all(data, 'tm', split_axis=0, concat_axis=0, tiled=True)  11.2 us
    pallas_call x1, Pallas kernels, by_baseline(): pl.pallas_call(kernel, in_specs=[pl.BlockSpec(memory_space=pl.ANY)], out_...  2.55 us
  transfers between devices with their start and end apart: 9, of which 6 were waited for; matrix products, arithmetic and copies ran while one was open for 2% of the time, Pallas kernels for 2%

profile of v4, /device:TPU:8, one launch (start us, length us, event | category | flops | bytes accessed | tf_op | source)
XLA Modules:
  0.0 122.6 jit_solution(17450371406851644813)
XLA Ops:
  0.0 2.5 %by_baseline.1 = bf16[32,128,256]{2,1,0:T(8,128)(2,1)} custom-call(bf16[128,64,128]{2,1,0:T(8,128)(2,1)} %in_ref.1), custom_call_target="tpu_custom_call" | custom-call | bytes 4194304 | tf_op jit(solution)/shard_map/by_baseline/pallas_call | solution.py:61
  2.6 0.0 copy-start.7
  2.6 0.0 copy-start.8
  2.6 14.0 %all-to-all-start = ((bf16[32,128,256]{2,1,0:T(8,128)(2,1)}), bf16[32,128,256]{2,1,0:T(8,128)(2,1)S(1)}, u32[]{:S(2)}, u32[]{:S(2)}) async-start(bf16[32,128,256]{2,1,0:T(8,128)(2,1)} %by_baseline.1), calls=%async_computation | async-start | bytes 4194304 | tf_op jit(solution)/shard_map/all_to_all | solution.py:222
  16.7 0.0 copy-done.7
  16.7 0.0 copy-done.8
  16.7 0.1 compare_convert_fusion
  16.8 1.8 %broadcast_multiply_fusion = bf16[16,64,1024]{2,1,0:T(8,128)(2,1)S(1)} fusion(bf16[16,64,1024]{2,1,0:T(8,128)(2,1)} %param.6, bf16[16,64]{1,0:T(8,128)(2,1)S(1)} %compare_convert_fusion), kind=kLoop, calls=%fused_computation | loop fusion | flops 1048576 | bytes 4196352 | tf_op jit(solution)/shard_map/mul | solution.py:226
  18.6 0.0 copy-start
  18.6 0.9 constant_dynamic-slice_fusion
  19.5 1.9 %collective-permute-start = (bf16[2,64,1024]{2,1,0:T(8,128)(2,1)S(1)}, bf16[2,64,1024]{2,1,0:T(8,128)(2,1)S(1)}, u32[]{:S(2)}, u32[]{:S(2)}) collective-permute-start(bf16[2,64,1024]{2,1,0:T(8,128)(2,1)S(1)} %get-tuple-element.29), channel_id=1, source_target_pairs={{0,1},{1,0},{4,5},{5,4},{8,9},{9,8},{12,13},{13,12},{2,3},{3,2},{6... | collective-permute-start | bytes 786440 | tf_op jit(solution)/shard_map/ppermute | solution.py:236
  21.4 3.4 %collective-permute-start.1 = (bf16[2,64,1024]{2,1,0:T(8,128)(2,1)S(1)}, bf16[2,64,1024]{2,1,0:T(8,128)(2,1)S(1)}, u32[]{:S(2)}, u32[]{:S(2)}) collective-permute-start(bf16[2,64,1024]{2,1,0:T(8,128)(2,1)S(1)} %get-tuple-element.28), channel_id=1, source_target_pairs={{0,4},{1,5},{4,8},{5,9},{8,12},{9,13},{12,0},{13,1},{2,6},{3,7},{6... | collective-permute-start | bytes 786440 | tf_op jit(solution)/shard_map/ppermute | solution.py:236
  24.8 3.2 %collective-permute-start.2 = (bf16[2,64,1024]{2,1,0:T(8,128)(2,1)S(1)}, bf16[2,64,1024]{2,1,0:T(8,128)(2,1)S(1)}, u32[]{:S(2)}, u32[]{:S(2)}) collective-permute-start(bf16[2,64,1024]{2,1,0:T(8,128)(2,1)S(1)} %get-tuple-element.27), channel_id=1, source_target_pairs={{0,5},{1,4},{4,9},{5,8},{8,13},{9,12},{12,1},{13,0},{2,7},{3,6},{6... | collective-permute-start | bytes 786440 | tf_op jit(solution)/shard_map/ppermute | solution.py:236
  28.0 3.6 %collective-permute-start.3 = (bf16[2,64,1024]{2,1,0:T(8,128)(2,1)S(1)}, bf16[2,64,1024]{2,1,0:T(8,128)(2,1)S(1)}, u32[]{:S(2)}, u32[]{:S(2)}) collective-permute-start(bf16[2,64,1024]{2,1,0:T(8,128)(2,1)S(1)} %get-tuple-element.26), channel_id=1, source_target_pairs={{0,8},{1,9},{4,12},{5,13},{8,0},{9,1},{12,4},{13,5},{2,10},{3,11},... | collective-permute-start | bytes 786440 | tf_op jit(solution)/shard_map/ppermute | solution.py:236
  31.7 3.3 %collective-permute-start.4 = (bf16[2,64,1024]{2,1,0:T(8,128)(2,1)S(1)}, bf16[2,64,1024]{2,1,0:T(8,128)(2,1)S(1)}, u32[]{:S(2)}, u32[]{:S(2)}) collective-permute-start(bf16[2,64,1024]{2,1,0:T(8,128)(2,1)S(1)} %get-tuple-element.25), channel_id=1, source_target_pairs={{0,9},{1,8},{4,13},{5,12},{8,1},{9,0},{12,5},{13,4},{2,11},{3,10},... | collective-permute-start | bytes 786440 | tf_op jit(solution)/shard_map/ppermute | solution.py:236
  35.0 0.0 collective-permute-done.refs_1_
  35.0 0.0 copy-start.1
  35.0 3.7 %collective-permute-start.5 = (bf16[2,64,1024]{2,1,0:T(8,128)(2,1)S(1)}, bf16[2,64,1024]{2,1,0:T(8,128)(2,1)S(1)}, u32[]{:S(2)}, u32[]{:S(2)}) collective-permute-start(bf16[2,64,1024]{2,1,0:T(8,128)(2,1)S(1)} %get-tuple-element.24), channel_id=1, source_target_pairs={{0,12},{1,13},{4,0},{5,1},{8,4},{9,5},{12,8},{13,9},{2,14},{3,15},... | collective-permute-start | bytes 786440 | tf_op jit(solution)/shard_map/ppermute | solution.py:236
  38.7 0.0 collective-permute-done.1.refs_2_
  38.7 0.0 copy-start.2
  38.7 2.3 %collective-permute-start.6 = (bf16[2,64,1024]{2,1,0:T(8,128)(2,1)S(1)}, bf16[2,64,1024]{2,1,0:T(8,128)(2,1)}, u32[]{:S(2)}, u32[]{:S(2)}) collective-permute-start(bf16[2,64,1024]{2,1,0:T(8,128)(2,1)S(1)} %get-tuple-element.23), channel_id=1, source_target_pairs={{0,13},{1,12},{4,1},{5,0},{8,5},{9,4},{12,9},{13,8},{2,15},{3,14},... | collective-permute-start | bytes 786440 | tf_op jit(solution)/shard_map/ppermute | solution.py:236
  41.0 0.0 collective-permute-done.2.refs_3_
  41.0 0.0 copy-start.3
  41.0 4.8 %collective-permute-done.3.refs_4_ = bf16[2,64,1024]{2,1,0:T(8,128)(2,1)S(1)} collective-permute-done((bf16[2,64,1024]{2,1,0:T(8,128)(2,1)S(1)}, bf16[2,64,1024]{2,1,0:T(8,128)(2,1)S(1)}, u32[]{:S(2)}, u32[]{:S(2)}) %collective-permute-start.3) | collective-permute-done | bytes 262176 | tf_op jit(solution)/shard_map/ppermute | solution.py:236
  45.8 0.0 copy-start.4
  45.8 4.8 %collective-permute-done.4.refs_5_ = bf16[2,64,1024]{2,1,0:T(8,128)(2,1)S(1)} collective-permute-done((bf16[2,64,1024]{2,1,0:T(8,128)(2,1)S(1)}, bf16[2,64,1024]{2,1,0:T(8,128)(2,1)S(1)}, u32[]{:S(2)}, u32[]{:S(2)}) %collective-permute-start.4) | collective-permute-done | bytes 262176 | tf_op jit(solution)/shard_map/ppermute | solution.py:236
  50.6 0.0 copy-start.5
  50.6 0.3 collective-permute-done.5.refs_6_
  50.9 0.0 copy-done.2
  50.9 0.0 copy-done.3
  50.9 0.0 copy-done.4
  50.9 0.4 copy-done.5
  51.3 0.0 copy-start.6
  51.3 0.7 copy-done.6
  52.1 3.3 %collective-permute-done.6.refs_7_ = bf16[2,64,1024]{2,1,0:T(8,128)(2,1)} collective-permute-done((bf16[2,64,1024]{2,1,0:T(8,128)(2,1)S(1)}, bf16[2,64,1024]{2,1,0:T(8,128)(2,1)}, u32[]{:S(2)}, u32[]{:S(2)}) %collective-permute-start.6) | collective-permute-done | bytes 262176 | tf_op jit(solution)/shard_map/ppermute | solution.py:236
  55.4 11.2 %all-to-all-done = bf16[32,128,256]{2,1,0:T(8,128)(2,1)S(1)} async-done(((bf16[32,128,256]{2,1,0:T(8,128)(2,1)}), bf16[32,128,256]{2,1,0:T(8,128)(2,1)S(1)}, u32[]{:S(2)}, u32[]{:S(2)}) %all-to-all-start) | async-done | bytes 2097184 | tf_op jit(solution)/shard_map/all_to_all | solution.py:222
  66.6 0.0 copy-done
  66.6 2.4 %transform.1.refs_8_ = bf16[1024,128]{1,0:T(8,128)(2,1)} custom-call(bf16[528,1024]{1,0:T(8,128)(2,1)S(1)} %copy-done, bf16[4096,256]{1,0:T(8,128)(2,1)S(1)} %bitcast.13), custom_call_target="tpu_custom_call" | custom-call | flops 1107296256 | bytes 3178496 | tf_op jit(solution)/shard_map/transform/pallas_call | solution.py:152
  69.1 0.0 copy-done.1
  69.1 13.1 %all-to-all-start.1 = ((bf16[256,4,128]{2,1,0:T(4,128)(2,1)}), bf16[256,4,128]{2,1,0:T(4,128)(2,1)S(1)}, u32[]{:S(2)}, u32[]{:S(2)}) async-start(bf16[256,4,128]{2,1,0:T(4,128)(2,1)} %bitcast.9), calls=%async_computation.1 | async-start | bytes 524288 | tf_op jit(solution)/shard_map/all_to_all | solution.py:243
  82.3 0.1 stack.35.sources_ref
  82.4 2.2 %prepare.1.inverse_ref = bf16[2,512,1024]{2,1,0:T(8,128)(2,1)S(1)} custom-call(bf16[2,64,1024]{2,1,0:T(8,128)(2,1)} %get-tuple-element.15.refs_0_, bf16[2,64,1024]{2,1,0:T(8,128)(2,1)} %copy-done.1, bf16[2,64,1024]{2,1,0:T(8,128)(2,1)} %copy-done.2, bf16[2,64,1024]{2,1,0:T(8,128)(2,1)} %copy-done.3, bf16[2,64,1024]{2,1,0:T(8,128)(2,1)} %copy-done.4, ...), custom_call_target="tpu_custom_call" | custom-call | bytes 4194304 | tf_op jit(solution)/shard_map/prepare/pallas_call | solution.py:95
  84.5 12.2 %all-to-all-done.1 = bf16[256,4,128]{2,1,0:T(4,128)(2,1)S(1)} async-done(((bf16[256,4,128]{2,1,0:T(4,128)(2,1)}), bf16[256,4,128]{2,1,0:T(4,128)(2,1)S(1)}, u32[]{:S(2)}, u32[]{:S(2)}) %all-to-all-start.1) | async-done | bytes 262176 | tf_op jit(solution)/shard_map/all_to_all | solution.py:243
  96.8 1.5 %product.1 = bf16[16,2,32,128]{3,2,1,0:T(8,128)(2,1)S(1)} custom-call(s32[8]{0:T(128)S(1)} %stack.35.sources_ref, bf16[1024,128]{1,0:T(8,128)(2,1)S(1)} %bitcast.14, bf16[2,512,1024]{2,1,0:T(8,128)(2,1)S(1)} %prepare.1.inverse_ref), custom_call_target="tpu_custom_call" | custom-call | flops 268435456 | bytes 2097152 | tf_op jit(solution)/shard_map/product/pallas_call | solution.py:190
  98.2 23.6 %all_to_all.21 = bf16[16,2,32,128]{3,2,1,0:T(8,128)(2,1)S(1)} all-to-all(bf16[16,2,32,128]{3,2,1,0:T(8,128)(2,1)S(1)} %product.1), channel_id=1, replica_groups=mesh['tm'=32,'x'=4,'h'=2,'c'=2] {'x','h','c'}, dimensions={0} | all-to-all | bytes 524288 | tf_op jit(solution)/shard_map/all_to_all | solution.py:246
  121.9 0.7 reduce
Async XLA Ops:
  2.6 14.1 %copy-start.7 = (s32[64]{0:T(128)S(1)}, s32[64]{0:T(128)}, u32[]{:S(2)}) copy-start(s32[64]{0:T(128)} %param.7) | copy-start | bytes 772
  2.6 14.1 %copy-start.8 = (s32[16]{0:T(128)S(1)}, s32[16]{0:T(128)}, u32[]{:S(2)}) copy-start(s32[16]{0:T(128)} %param.8) | copy-start | bytes 196
  2.6 64.0 %all-to-all-start = ((bf16[32,128,256]{2,1,0:T(8,128)(2,1)}), bf16[32,128,256]{2,1,0:T(8,128)(2,1)S(1)}, u32[]{:S(2)}, u32[]{:S(2)}) async-start(bf16[32,128,256]{2,1,0:T(8,128)(2,1)} %by_baseline.1), calls=%async_computation | async-start | bytes 4194304 | tf_op jit(solution)/shard_map/all_to_all | solution.py:222
  18.6 48.1 %copy-start = (bf16[528,1024]{1,0:T(8,128)(2,1)S(1)}, bf16[528,1024]{1,0:T(8,128)(2,1)}, u32[]{:S(2)}) copy-start(bf16[528,1024]{1,0:T(8,128)(2,1)} %constant.124.clone.table_ref) | copy-start | bytes 3244036
  19.5 15.5 %collective-permute-start = (bf16[2,64,1024]{2,1,0:T(8,128)(2,1)S(1)}, bf16[2,64,1024]{2,1,0:T(8,128)(2,1)S(1)}, u32[]{:S(2)}, u32[]{:S(2)}) collective-permute-start(bf16[2,64,1024]{2,1,0:T(8,128)(2,1)S(1)} %get-tuple-element.29), channel_id=1, source_target_pairs={{0,1},{1,0},{4,5},{5,4},{8,9},{9,8},{12,13},{13,12},{2,3},{3,2},{6... | collective-permute-start | bytes 786440 | tf_op jit(solution)/shard_map/ppermute | solution.py:236
  21.4 17.3 %collective-permute-start.1 = (bf16[2,64,1024]{2,1,0:T(8,128)(2,1)S(1)}, bf16[2,64,1024]{2,1,0:T(8,128)(2,1)S(1)}, u32[]{:S(2)}, u32[]{:S(2)}) collective-permute-start(bf16[2,64,1024]{2,1,0:T(8,128)(2,1)S(1)} %get-tuple-element.28), channel_id=1, source_target_pairs={{0,4},{1,5},{4,8},{5,9},{8,12},{9,13},{12,0},{13,1},{2,6},{3,7},{6... | collective-permute-start | bytes 786440 | tf_op jit(solution)/shard_map/ppermute | solution.py:236
  24.8 16.2 %collective-permute-start.2 = (bf16[2,64,1024]{2,1,0:T(8,128)(2,1)S(1)}, bf16[2,64,1024]{2,1,0:T(8,128)(2,1)S(1)}, u32[]{:S(2)}, u32[]{:S(2)}) collective-permute-start(bf16[2,64,1024]{2,1,0:T(8,128)(2,1)S(1)} %get-tuple-element.27), channel_id=1, source_target_pairs={{0,5},{1,4},{4,9},{5,8},{8,13},{9,12},{12,1},{13,0},{2,7},{3,6},{6... | collective-permute-start | bytes 786440 | tf_op jit(solution)/shard_map/ppermute | solution.py:236
  28.0 17.8 %collective-permute-start.3 = (bf16[2,64,1024]{2,1,0:T(8,128)(2,1)S(1)}, bf16[2,64,1024]{2,1,0:T(8,128)(2,1)S(1)}, u32[]{:S(2)}, u32[]{:S(2)}) collective-permute-start(bf16[2,64,1024]{2,1,0:T(8,128)(2,1)S(1)} %get-tuple-element.26), channel_id=1, source_target_pairs={{0,8},{1,9},{4,12},{5,13},{8,0},{9,1},{12,4},{13,5},{2,10},{3,11},... | collective-permute-start | bytes 786440 | tf_op jit(solution)/shard_map/ppermute | solution.py:236
  31.7 19.0 %collective-permute-start.4 = (bf16[2,64,1024]{2,1,0:T(8,128)(2,1)S(1)}, bf16[2,64,1024]{2,1,0:T(8,128)(2,1)S(1)}, u32[]{:S(2)}, u32[]{:S(2)}) collective-permute-start(bf16[2,64,1024]{2,1,0:T(8,128)(2,1)S(1)} %get-tuple-element.25), channel_id=1, source_target_pairs={{0,9},{1,8},{4,13},{5,12},{8,1},{9,0},{12,5},{13,4},{2,11},{3,10},... | collective-permute-start | bytes 786440 | tf_op jit(solution)/shard_map/ppermute | solution.py:236
  35.0 34.0 %copy-start.1 = (bf16[2,64,1024]{2,1,0:T(8,128)(2,1)}, bf16[2,64,1024]{2,1,0:T(8,128)(2,1)S(1)}, u32[]{:S(2)}) copy-start(bf16[2,64,1024]{2,1,0:T(8,128)(2,1)S(1)} %collective-permute-done.refs_1_) | copy-start | bytes 786436
  35.0 15.9 %collective-permute-start.5 = (bf16[2,64,1024]{2,1,0:T(8,128)(2,1)S(1)}, bf16[2,64,1024]{2,1,0:T(8,128)(2,1)S(1)}, u32[]{:S(2)}, u32[]{:S(2)}) collective-permute-start(bf16[2,64,1024]{2,1,0:T(8,128)(2,1)S(1)} %get-tuple-element.24), channel_id=1, source_target_pairs={{0,12},{1,13},{4,0},{5,1},{8,4},{9,5},{12,8},{13,9},{2,14},{3,15},... | collective-permute-start | bytes 786440 | tf_op jit(solution)/shard_map/ppermute | solution.py:236
  38.7 12.2 %copy-start.2 = (bf16[2,64,1024]{2,1,0:T(8,128)(2,1)}, bf16[2,64,1024]{2,1,0:T(8,128)(2,1)S(1)}, u32[]{:S(2)}) copy-start(bf16[2,64,1024]{2,1,0:T(8,128)(2,1)S(1)} %collective-permute-done.1.refs_2_) | copy-start | bytes 786436
  38.7 16.7 %collective-permute-start.6 = (bf16[2,64,1024]{2,1,0:T(8,128)(2,1)S(1)}, bf16[2,64,1024]{2,1,0:T(8,128)(2,1)}, u32[]{:S(2)}, u32[]{:S(2)}) collective-permute-start(bf16[2,64,1024]{2,1,0:T(8,128)(2,1)S(1)} %get-tuple-element.23), channel_id=1, source_target_pairs={{0,13},{1,12},{4,1},{5,0},{8,5},{9,4},{12,9},{13,8},{2,15},{3,14},... | collective-permute-start | bytes 786440 | tf_op jit(solution)/shard_map/ppermute | solution.py:236
  41.0 9.9 %copy-start.3 = (bf16[2,64,1024]{2,1,0:T(8,128)(2,1)}, bf16[2,64,1024]{2,1,0:T(8,128)(2,1)S(1)}, u32[]{:S(2)}) copy-start(bf16[2,64,1024]{2,1,0:T(8,128)(2,1)S(1)} %collective-permute-done.2.refs_3_) | copy-start | bytes 786436
  45.8 5.1 %copy-start.4 = (bf16[2,64,1024]{2,1,0:T(8,128)(2,1)}, bf16[2,64,1024]{2,1,0:T(8,128)(2,1)S(1)}, u32[]{:S(2)}) copy-start(bf16[2,64,1024]{2,1,0:T(8,128)(2,1)S(1)} %collective-permute-done.3.refs_4_) | copy-start | bytes 786436
  50.6 0.7 copy-start.5
  51.3 0.7 copy-start.6
  69.1 27.7 %all-to-all-start.1 = ((bf16[256,4,128]{2,1,0:T(4,128)(2,1)}), bf16[256,4,128]{2,1,0:T(4,128)(2,1)S(1)}, u32[]{:S(2)}, u32[]{:S(2)}) async-start(bf16[256,4,128]{2,1,0:T(4,128)(2,1)} %bitcast.9), calls=%async_computation.1 | async-start | bytes 524288 | tf_op jit(solution)/shard_map/all_to_all | solution.py:243
